TPU v7x, 128 devices: a whole 4x4x4 slice. The times are simulated.
128 devices in a mesh: gx: 4 (over y_hi, core), gy: 32 (over y_lo, z, x).
Axes of the slice: x: 4, y: 4 (y_hi: 2, y_lo: 2; y = y_hi * 2 + y_lo), z: 4, core: 2. Of those that a mesh axis runs over, the one named last changes fastest.
Arguments:
- inputs: bfloat16 [256, 256, 384], P('gx', 'gy'), may hold values from -6 to 6
- norm_gains: float32 [4, 384], replicated, may hold values from 0.5 to 1.5
- weights: bfloat16 [4, 3456, 384], replicated, may hold values from -0.109375 to 0.109375
- cotangent: float32 [256, 256, 384], P('gx', 'gy'), may hold values from -6 to 6
Outputs:
- outputs: float32 [256, 256, 384], P('gx', 'gy')
- input_grad: float32 [256, 256, 384], P('gx', 'gy')
- weight_grads: float32 [4, 1327104], P(None, ('gx', 'gy'))
All inputs are finite; a program needn't handle non-finite values.
Results may differ from a plain program's by a relative error of at most 0.0048.
Values may be sent and summed in bfloat16 or wider, within the bound.
A program may use at most 192 MiB of HBM per device.

v0:
```python
from functools import partial
import math

import jax
import jax.numpy as jnp
from jax import lax
from jax.sharding import PartitionSpec as P

DILATIONS = (1, 4, 32, 128)
OFFSETS = tuple(((row_step, col_step) for row_step in (-1, 0, 1) for col_step in (-1, 0, 1)))
EPSILON = 1e-05


def with_halo(block, sides, width):
    for axis, dim in sides:
        count = lax.axis_size(axis)
        forward = [(i, i + 1) for i in range(count - 1)]
        backward = [(target, source) for source, target in forward]
        low = lax.ppermute(
            lax.slice_in_dim(block, block.shape[dim] - width, None, axis=dim), axis, forward
        )
        high = lax.ppermute(lax.slice_in_dim(block, 0, width, axis=dim), axis, backward)
        block = jnp.concatenate([low, block, high], axis=dim)
    return block


def passed_along(shard, axis, by):
    length = lax.axis_size(axis)
    pairs = [(i, i + by) for i in range(length) if 0 <= i + by < length]
    return lax.ppermute(shard, axis, pairs)


def norm_act(stream, gain_row):
    average = jnp.mean(stream, axis=-1, keepdims=True)
    centred = stream - average
    spread = jnp.mean(centred * centred, axis=-1, keepdims=True)
    return jax.nn.gelu(centred * lax.rsqrt(spread + EPSILON) * gain_row)


def tile_near(source, dilation):
    rows_here, cols_here = (source.shape[0], source.shape[1])
    padded = with_halo(source, (("gx", 0), ("gy", 1)), dilation)
    pieces = []
    for row_step, col_step in OFFSETS:
        top_row = dilation + row_step * dilation
        left_col = dilation + col_step * dilation
        pieces.append(padded[top_row : top_row + rows_here, left_col : left_col + cols_here])
    return pieces


def fetch_rows(source, devices_away):
    if devices_away == 0:
        return source
    return passed_along(source, "gx", -devices_away)


def fetch_cols(source, devices_away):
    if devices_away == 0:
        return source
    return passed_along(source, "gy", -devices_away)


def move_rows(source, cells):
    extent = source.shape[0]
    whole, rest = divmod(cells, extent)
    first = fetch_rows(source, whole)
    if rest == 0:
        return first
    second = fetch_rows(source, whole + 1)
    return jnp.concatenate([first[rest:], second[:rest]], axis=0)


def move_cols(source, cells):
    extent = source.shape[1]
    whole, rest = divmod(cells, extent)
    first = fetch_cols(source, whole)
    return first


def tile_far(source, dilation):
    versions = {}
    for row_step in (-1, 0, 1):
        versions[row_step] = move_rows(source, row_step * dilation)
    pieces = []
    for row_step, col_step in OFFSETS:
        pieces.append(move_cols(versions[row_step], col_step * dilation))
    return pieces


def forward_block(stream, gain_row, weight_block, taps):
    channels = stream.shape[-1]
    acted = norm_act(stream, gain_row).astype(jnp.bfloat16)
    patches = jnp.concatenate([piece.reshape(-1, channels) for piece in taps(acted)], axis=1)
    update = jnp.dot(patches, weight_block, preferred_element_type=jnp.float32)
    return (stream + update.reshape(stream.shape), patches)


def backward_block(stream, grad, gain_row, weight_block, patches, taps, scale):
    channels = stream.shape[-1]
    g_out = grad.astype(jnp.bfloat16)
    flat_grad = g_out.reshape(-1, channels)
    local_term = lax.dot_general(
        patches, flat_grad, (((0,), (0,)), ((), ())), preferred_element_type=jnp.float32
    )
    grad_share = lax.psum_scatter(
        local_term.reshape(-1) * scale, ("gx", "gy"), scatter_dimension=0, tiled=True
    )
    pieces = taps(g_out)[::-1]
    back_taps = jnp.stack([piece.reshape(-1, channels) for piece in pieces], axis=1)
    kernel = weight_block.reshape(9, channels, channels)
    d_act = lax.dot_general(
        back_taps, kernel, (((1, 2), (0, 2)), ((), ())), preferred_element_type=jnp.float32
    )
    _, pullback = jax.vjp(lambda state_in: norm_act(state_in, gain_row), stream)
    return (grad + pullback(d_act.reshape(stream.shape))[0], grad_share)


def body(inputs, norm_gains, weights, cotangent):
    rows_here, cols_here, channels = inputs.shape
    rows_axis = lax.axis_size("gx")
    cols_axis = lax.axis_size("gy")
    scale = 1.0 / math.sqrt(rows_here * cols_here * rows_axis * cols_axis)
    shares = [None] * 4
    stream = inputs.astype(jnp.float32)
    near_saved = []
    for block_index in range(2):
        taps = partial(tile_near, dilation=DILATIONS[block_index])
        near_saved.append(stream)
        stream, patches = forward_block(stream, norm_gains[block_index], weights[block_index], taps)
        near_saved.append(patches)
    far_saved = {}
    for block_index in (2, 3):
        taps = partial(tile_far, dilation=DILATIONS[block_index])
        before = stream
        stream, patches = forward_block(stream, norm_gains[block_index], weights[block_index], taps)
        far_saved[block_index] = (before, patches, taps)
    grad = cotangent
    for block_index in (3, 2):
        before, patches, taps = far_saved[block_index]
        grad, shares[block_index] = backward_block(
            before, grad, norm_gains[block_index], weights[block_index], patches, taps, scale
        )
    for block_index in (1, 0):
        taps = partial(tile_near, dilation=DILATIONS[block_index])
        before = near_saved[2 * block_index]
        patches = near_saved[2 * block_index + 1]
        grad, shares[block_index] = backward_block(
            before, grad, norm_gains[block_index], weights[block_index], patches, taps, scale
        )
    return (stream, grad, jnp.stack(shares))


def solution(mesh):
    placed = (P("gx", "gy", None), P(), P(), P("gx", "gy", None))
    return jax.shard_map(
        body,
        mesh=mesh,
        in_specs=placed,
        out_specs=(P("gx", "gy", None), P("gx", "gy", None), P(None, ("gx", "gy"))),
        check_vma=False,
    )
```

profile of v0, /device:TPU:0, one launch (start us, length us, event | category | flops | bytes accessed | tf_op | source)
XLA Modules:
  0.0 542.8 jit_solution(16466128806758700958)
XLA Ops:
  20.1 4.6 collective-permute-start.28
  26.5 4.8 collective-permute-start.2
  31.3 7.2 %fusion.103 = (bf16[1,3456,384]{2,1,0:T(8,128)(2,1)}, bf16[1,3456,384]{2,1,0:T(8,128)(2,1)}, bf16[1,3456,384]{2,1,0:T(8,128)(2,1)S(1)}, bf16[1,3456,384]{2,1,0:T(8,128)(2,1)}) fusion(bf16[4,3456,384]{2,1,0:T(8,128)(2,1)} %param.6), kind=kLoop, calls=%fused_computation.282 | loop fusion | bytes 21233664 | tf_op jit(solution)/shard_map/slice | solution.py:129
  51.8 4.8 collective-permute-start.6
  73.0 10.6 %collective-permute-start.29 = (bf16[64,8,384]{2,1,0:T(8,128)(2,1)S(1)}, bf16[64,8,384]{2,1,0:T(8,128)(2,1)S(1)}, u32[]{:S(2)}, u32[]{:S(2)}) collective-permute-start(bf16[64,8,384]{2,1,0:T(8,128)(2,1)S(1)} %convert_element_type.32), channel_id=1, source_target_pairs={{0,64},{32,96},{1,65},{33,97},{2,66},{34,98},{3,67},{35,99},{4,68}... | collective-permute-start | bytes 1179656 | tf_op jit(solution)/shard_map/ppermute | solution.py:30
  83.7 10.8 %collective-permute-start.11 = (bf16[64,8,384]{2,1,0:T(8,128)(2,1)S(1)}, bf16[64,8,384]{2,1,0:T(8,128)(2,1)S(1)}, u32[]{:S(2)}, u32[]{:S(2)}) collective-permute-start(bf16[64,8,384]{2,1,0:T(8,128)(2,1)S(1)} %multiply_convert_fusion.1), channel_id=1, source_target_pairs={{0,4},{1,5},{2,6},{3,7},{4,8},{5,9},{6,10},{7,11},{8,12},{9,13},{1... | collective-permute-start | bytes 1179656 | tf_op jit(solution)/shard_map/ppermute | solution.py:30
  94.7 4.5 collective-permute-done.25
  99.2 8.0 %collective-permute-start.26 = (bf16[64,8,384]{2,1,0:T(8,128)(2,1)S(1)}, bf16[64,8,384]{2,1,0:T(8,128)(2,1)S(1)}, u32[]{:S(2)}, u32[]{:S(2)}) collective-permute-start(bf16[64,8,384]{2,1,0:T(8,128)(2,1)S(1)} %collective-permute-done.24), channel_id=1, source_target_pairs={{0,16},{1,17},{2,18},{3,19},{4,20},{5,21},{6,22},{7,23},{8,24},{9,... | collective-permute-start | bytes 1179656 | tf_op jit(solution)/shard_map/ppermute | solution.py:30
  108.6 7.3 %collective-permute-done.26 = bf16[64,8,384]{2,1,0:T(8,128)(2,1)S(1)} collective-permute-done((bf16[64,8,384]{2,1,0:T(8,128)(2,1)S(1)}, bf16[64,8,384]{2,1,0:T(8,128)(2,1)S(1)}, u32[]{:S(2)}, u32[]{:S(2)}) %collective-permute-start.26) | collective-permute-done | bytes 393248 | tf_op jit(solution)/shard_map/ppermute | solution.py:30
  117.2 4.6 collective-permute-start.31
  123.4 6.6 %collective-permute-done.30 = bf16[64,8,384]{2,1,0:T(8,128)(2,1)S(1)} collective-permute-done((bf16[64,8,384]{2,1,0:T(8,128)(2,1)S(1)}, bf16[64,8,384]{2,1,0:T(8,128)(2,1)S(1)}, u32[]{:S(2)}, u32[]{:S(2)}) %collective-permute-start.30) | collective-permute-done | bytes 393248 | tf_op jit(solution)/shard_map/ppermute | solution.py:30
  131.5 4.6 collective-permute-start.14
  137.8 6.2 %collective-permute-done.10 = bf16[64,8,384]{2,1,0:T(8,128)(2,1)S(1)} collective-permute-done((bf16[64,8,384]{2,1,0:T(8,128)(2,1)S(1)}, bf16[64,8,384]{2,1,0:T(8,128)(2,1)S(1)}, u32[]{:S(2)}, u32[]{:S(2)}) %collective-permute-start.10) | collective-permute-done | bytes 393248 | tf_op jit(solution)/shard_map/ppermute | solution.py:30
  144.9 5.6 %collective-permute-done.15 = bf16[64,8,384]{2,1,0:T(8,128)(2,1)S(1)} collective-permute-done((bf16[64,8,384]{2,1,0:T(8,128)(2,1)S(1)}, bf16[64,8,384]{2,1,0:T(8,128)(2,1)S(1)}, u32[]{:S(2)}, u32[]{:S(2)}) %collective-permute-start.15) | collective-permute-done | bytes 393248 | tf_op jit(solution)/shard_map/ppermute | solution.py:30
  160.0 10.8 %collective-permute-start.19 = (bf16[64,8,384]{2,1,0:T(8,128)(2,1)S(1)}, bf16[64,8,384]{2,1,0:T(8,128)(2,1)}, u32[]{:S(2)}, u32[]{:S(2)}) collective-permute-start(bf16[64,8,384]{2,1,0:T(8,128)(2,1)S(1)} %get-tuple-element.21), channel_id=1, source_target_pairs={{0,16},{1,17},{2,18},{3,19},{4,20},{5,21},{6,22},{7,23},{8,24},{9,... | collective-permute-start | bytes 1179656 | tf_op jit(solution)/shard_map/ppermute | solution.py:30
  181.4 4.5 convolution_multiply_fusion.1
  185.8 6.6 %mul.544 = f32[1327104]{0:T(1024)} reshape(f32[3456,384]{1,0:T(8,128)} %convolution_multiply_fusion.1) | data formatting | bytes 10616832 | tf_op jit(solution)/shard_map/mul | solution.py:106
  192.4 4.7 collective-permute-start.34
  202.8 4.6 collective-permute-start.36
  212.6 4.4 collective-permute-start.39
  218.7 5.4 collective-permute-start.17
  225.6 7.7 %collective-permute-start.22 = (bf16[64,8,384]{2,1,0:T(8,128)(2,1)}, bf16[64,8,384]{2,1,0:T(8,128)(2,1)S(1)}, u32[]{:S(2)}, u32[]{:S(2)}) collective-permute-start(bf16[64,8,384]{2,1,0:T(8,128)(2,1)} %collective-permute-done.21), channel_id=1, source_target_pairs={{0,16},{1,17},{2,18},{3,19},{4,20},{5,21},{6,22},{7,23},{8,24},{9,... | collective-permute-start | bytes 1179656 | tf_op jit(solution)/shard_map/ppermute | solution.py:30
  242.0 8.0 %collective-permute-start.40 = (bf16[4,8,384]{2,1,0:T(8,128)(2,1)S(1)}, bf16[4,8,384]{2,1,0:T(8,128)(2,1)S(1)}, u32[]{:S(2)}, u32[]{:S(2)}) collective-permute-start(bf16[4,8,384]{2,1,0:T(8,128)(2,1)S(1)} %get-tuple-element.40), channel_id=1, source_target_pairs={{0,32},{32,64},{64,96},{1,33},{33,65},{65,97},{2,34},{34,66},{66,9... | collective-permute-start | bytes 73736 | tf_op jit(solution)/shard_map/ppermute | solution.py:19
  253.4 4.4 convolution_multiply_fusion
  260.8 4.4 convolution_multiply_fusion.2
  265.2 6.6 %mul.546 = f32[1327104]{0:T(1024)} reshape(f32[3456,384]{1,0:T(8,128)} %convolution_multiply_fusion) | data formatting | bytes 10616832 | tf_op jit(solution)/shard_map/mul | solution.py:106
  271.8 6.6 %mul.542 = f32[1327104]{0:T(1024)} reshape(f32[3456,384]{1,0:T(8,128)} %convolution_multiply_fusion.2) | data formatting | bytes 10616832 | tf_op jit(solution)/shard_map/mul | solution.py:106
  285.4 4.4 convolution_multiply_fusion.3
  289.8 6.6 %mul.540 = f32[1327104]{0:T(1024)} reshape(f32[3456,384]{1,0:T(8,128)} %convolution_multiply_fusion.3) | data formatting | bytes 10616832 | tf_op jit(solution)/shard_map/mul | solution.py:106
  303.4 7.4 %collective-permute-start.44 = (bf16[1,8,384]{2,1,0:T(8,128)(2,1)S(1)}, bf16[1,8,384]{2,1,0:T(8,128)(2,1)S(1)}, u32[]{:S(2)}, u32[]{:S(2)}) collective-permute-start(bf16[1,8,384]{2,1,0:T(8,128)(2,1)S(1)} %get-tuple-element.38), channel_id=1, source_target_pairs={{0,32},{32,64},{64,96},{1,33},{33,65},{65,97},{2,34},{34,66},{66,9... | collective-permute-start | bytes 18440 | tf_op jit(solution)/shard_map/ppermute | solution.py:19
  317.5 4.8 fusion.17
  329.9 201.3 %all-reduce.7.cloned.1.call-done = (f32[1327104]{0:T(1024)}, f32[1327104]{0:T(1024)}, f32[1327104]{0:T(1024)}, f32[1327104]{0:T(1024)}) async-done(((f32[1327104]{0:T(1024)}, f32[1327104]{0:T(1024)}, f32[1327104]{0:T(1024)}, f32[1327104]{0:T(1024)}), (f32[1327104]{0:T(1024)}, f32[1327104]{0:T(1024)}, f32[1327104]{0:T(1024)}, f32[1327104]{0:T(1024)})) %all-reduce.7.cloned.1.call-update) | async-done | bytes 21233680
  (366 shorter events, 132.9 us)
Async XLA Ops:
  7.2 524.0 %all-reduce.7.cloned.1.call-start = ((), (), s32[]{:S(2)}) async-start(), calls=%async_computation | async-start | bytes 42467328
  17.5 54.0 %collective-permute-start.24 = (bf16[64,8,384]{2,1,0:T(8,128)(2,1)S(1)}, bf16[64,8,384]{2,1,0:T(8,128)(2,1)S(1)}, u32[]{:S(2)}, u32[]{:S(2)}) collective-permute-start(bf16[64,8,384]{2,1,0:T(8,128)(2,1)S(1)} %convert_element_type.32), channel_id=1, source_target_pairs={{64,0},{96,32},{65,1},{97,33},{66,2},{98,34},{67,3},{99,35},{68,4}... | collective-permute-start | bytes 1179656 | tf_op jit(solution)/shard_map/ppermute | solution.py:30
  18.8 98.4 %collective-permute-start.27 = (bf16[64,8,384]{2,1,0:T(8,128)(2,1)S(1)}, bf16[64,8,384]{2,1,0:T(8,128)(2,1)S(1)}, u32[]{:S(2)}, u32[]{:S(2)}) collective-permute-start(bf16[64,8,384]{2,1,0:T(8,128)(2,1)S(1)} %convert_element_type.32), channel_id=1, source_target_pairs={{16,0},{17,1},{18,2},{19,3},{20,4},{21,5},{22,6},{23,7},{24,8},{25... | collective-permute-start | bytes 1179656 | tf_op jit(solution)/shard_map/ppermute | solution.py:30
  20.1 101.9 %collective-permute-start.28 = (bf16[64,8,384]{2,1,0:T(8,128)(2,1)S(1)}, bf16[64,8,384]{2,1,0:T(8,128)(2,1)S(1)}, u32[]{:S(2)}, u32[]{:S(2)}) collective-permute-start(bf16[64,8,384]{2,1,0:T(8,128)(2,1)S(1)} %convert_element_type.32), channel_id=1, source_target_pairs={{0,16},{1,17},{2,18},{3,19},{4,20},{5,21},{6,22},{7,23},{8,24},{9,... | collective-permute-start | bytes 1179656 | tf_op jit(solution)/shard_map/ppermute | solution.py:30
  24.9 13.6 %collective-permute-start.3 = (bf16[66,1,384]{2,1,0:T(2,128)(2,1)S(1)}, bf16[66,1,384]{2,1,0:T(2,128)(2,1)S(1)}, u32[]{:S(2)}, u32[]{:S(2)}) collective-permute-start(bf16[66,1,384]{2,1,0:T(2,128)(2,1)S(1)} %get-tuple-element.36), channel_id=1, source_target_pairs={{1,0},{2,1},{3,2},{4,3},{5,4},{6,5},{7,6},{8,7},{9,8},{10,9},{11,1... | collective-permute-start | bytes 152072 | tf_op jit(solution)/shard_map/ppermute | solution.py:22
  68.8 14.8 %collective-permute-start.13 = (bf16[64,8,384]{2,1,0:T(8,128)(2,1)S(1)}, bf16[64,8,384]{2,1,0:T(8,128)(2,1)S(1)}, u32[]{:S(2)}, u32[]{:S(2)}) collective-permute-start(bf16[64,8,384]{2,1,0:T(8,128)(2,1)S(1)} %multiply_convert_fusion.1), channel_id=1, source_target_pairs={{32,0},{64,32},{96,64},{33,1},{65,33},{97,65},{34,2},{66,34},{98,6... | collective-permute-start | bytes 1179656 | tf_op jit(solution)/shard_map/ppermute | solution.py:30
  71.5 27.6 %collective-permute-start.25 = (bf16[64,8,384]{2,1,0:T(8,128)(2,1)S(1)}, bf16[64,8,384]{2,1,0:T(8,128)(2,1)S(1)}, u32[]{:S(2)}, u32[]{:S(2)}) collective-permute-start(bf16[64,8,384]{2,1,0:T(8,128)(2,1)S(1)} %collective-permute-done.24), channel_id=1, source_target_pairs={{16,0},{17,1},{18,2},{19,3},{20,4},{21,5},{22,6},{23,7},{24,8},{25... | collective-permute-start | bytes 1179656 | tf_op jit(solution)/shard_map/ppermute | solution.py:30
  73.0 34.2 %collective-permute-start.29 = (bf16[64,8,384]{2,1,0:T(8,128)(2,1)S(1)}, bf16[64,8,384]{2,1,0:T(8,128)(2,1)S(1)}, u32[]{:S(2)}, u32[]{:S(2)}) collective-permute-start(bf16[64,8,384]{2,1,0:T(8,128)(2,1)S(1)} %convert_element_type.32), channel_id=1, source_target_pairs={{0,64},{32,96},{1,65},{33,97},{2,66},{34,98},{3,67},{35,99},{4,68}... | collective-permute-start | bytes 1179656 | tf_op jit(solution)/shard_map/ppermute | solution.py:30
  83.7 60.4 %collective-permute-start.11 = (bf16[64,8,384]{2,1,0:T(8,128)(2,1)S(1)}, bf16[64,8,384]{2,1,0:T(8,128)(2,1)S(1)}, u32[]{:S(2)}, u32[]{:S(2)}) collective-permute-start(bf16[64,8,384]{2,1,0:T(8,128)(2,1)S(1)} %multiply_convert_fusion.1), channel_id=1, source_target_pairs={{0,4},{1,5},{2,6},{3,7},{4,8},{5,9},{6,10},{7,11},{8,12},{9,13},{1... | collective-permute-start | bytes 1179656 | tf_op jit(solution)/shard_map/ppermute | solution.py:30
  99.2 16.7 %collective-permute-start.26 = (bf16[64,8,384]{2,1,0:T(8,128)(2,1)S(1)}, bf16[64,8,384]{2,1,0:T(8,128)(2,1)S(1)}, u32[]{:S(2)}, u32[]{:S(2)}) collective-permute-start(bf16[64,8,384]{2,1,0:T(8,128)(2,1)S(1)} %collective-permute-done.24), channel_id=1, source_target_pairs={{0,16},{1,17},{2,18},{3,19},{4,20},{5,21},{6,22},{7,23},{8,24},{9,... | collective-permute-start | bytes 1179656 | tf_op jit(solution)/shard_map/ppermute | solution.py:30
  107.3 37.4 %collective-permute-start.12 = (bf16[64,8,384]{2,1,0:T(8,128)(2,1)S(1)}, bf16[64,8,384]{2,1,0:T(8,128)(2,1)S(1)}, u32[]{:S(2)}, u32[]{:S(2)}) collective-permute-start(bf16[64,8,384]{2,1,0:T(8,128)(2,1)S(1)} %multiply_convert_fusion.1), channel_id=1, source_target_pairs={{4,0},{5,1},{6,2},{7,3},{8,4},{9,5},{10,6},{11,7},{12,8},{13,9},{1... | collective-permute-start | bytes 1179656 | tf_op jit(solution)/shard_map/ppermute | solution.py:30
  115.9 14.2 %collective-permute-start.30 = (bf16[64,8,384]{2,1,0:T(8,128)(2,1)S(1)}, bf16[64,8,384]{2,1,0:T(8,128)(2,1)S(1)}, u32[]{:S(2)}, u32[]{:S(2)}) collective-permute-start(bf16[64,8,384]{2,1,0:T(8,128)(2,1)S(1)} %collective-permute-done.29), channel_id=1, source_target_pairs={{16,0},{17,1},{18,2},{19,3},{20,4},{21,5},{22,6},{23,7},{24,8},{25... | collective-permute-start | bytes 1179656 | tf_op jit(solution)/shard_map/ppermute | solution.py:30
  117.2 14.2 %collective-permute-start.31 = (bf16[64,8,384]{2,1,0:T(8,128)(2,1)S(1)}, bf16[64,8,384]{2,1,0:T(8,128)(2,1)S(1)}, u32[]{:S(2)}, u32[]{:S(2)}) collective-permute-start(bf16[64,8,384]{2,1,0:T(8,128)(2,1)S(1)} %collective-permute-done.29), channel_id=1, source_target_pairs={{0,16},{1,17},{2,18},{3,19},{4,20},{5,21},{6,22},{7,23},{8,24},{9,... | collective-permute-start | bytes 1179656 | tf_op jit(solution)/shard_map/ppermute | solution.py:30
  122.0 14.1 %collective-permute-start.9 = (bf16[64,8,384]{2,1,0:T(8,128)(2,1)S(1)}, bf16[64,8,384]{2,1,0:T(8,128)(2,1)S(1)}, u32[]{:S(2)}, u32[]{:S(2)}) collective-permute-start(bf16[64,8,384]{2,1,0:T(8,128)(2,1)S(1)} %pad_maximum_fusion.14), channel_id=1, source_target_pairs={{0,4},{1,5},{2,6},{3,7},{4,8},{5,9},{6,10},{7,11},{8,12},{9,13},{1... | collective-permute-start | bytes 1179656 | tf_op jit(solution)/shard_map/ppermute | solution.py:30
  130.0 13.9 %collective-permute-start.10 = (bf16[64,8,384]{2,1,0:T(8,128)(2,1)S(1)}, bf16[64,8,384]{2,1,0:T(8,128)(2,1)S(1)}, u32[]{:S(2)}, u32[]{:S(2)}) collective-permute-start(bf16[64,8,384]{2,1,0:T(8,128)(2,1)S(1)} %pad_maximum_fusion.14), channel_id=1, source_target_pairs={{4,0},{5,1},{6,2},{7,3},{8,4},{9,5},{10,6},{11,7},{12,8},{13,9},{1... | collective-permute-start | bytes 1179656 | tf_op jit(solution)/shard_map/ppermute | solution.py:30
  131.5 13.2 %collective-permute-start.14 = (bf16[64,8,384]{2,1,0:T(8,128)(2,1)S(1)}, bf16[64,8,384]{2,1,0:T(8,128)(2,1)S(1)}, u32[]{:S(2)}, u32[]{:S(2)}) collective-permute-start(bf16[64,8,384]{2,1,0:T(8,128)(2,1)S(1)} %pad_maximum_fusion.15), channel_id=1, source_target_pairs={{0,4},{1,5},{2,6},{3,7},{4,8},{5,9},{6,10},{7,11},{8,12},{9,13},{1... | collective-permute-start | bytes 1179656 | tf_op jit(solution)/shard_map/ppermute | solution.py:30
  136.1 14.3 %collective-permute-start.15 = (bf16[64,8,384]{2,1,0:T(8,128)(2,1)S(1)}, bf16[64,8,384]{2,1,0:T(8,128)(2,1)S(1)}, u32[]{:S(2)}, u32[]{:S(2)}) collective-permute-start(bf16[64,8,384]{2,1,0:T(8,128)(2,1)S(1)} %pad_maximum_fusion.15), channel_id=1, source_target_pairs={{4,0},{5,1},{6,2},{7,3},{8,4},{9,5},{10,6},{11,7},{12,8},{13,9},{1... | collective-permute-start | bytes 1179656 | tf_op jit(solution)/shard_map/ppermute | solution.py:30
  156.2 60.9 %collective-permute-start.16 = (bf16[64,8,384]{2,1,0:T(8,128)(2,1)S(1)}, bf16[64,8,384]{2,1,0:T(8,128)(2,1)}, u32[]{:S(2)}, u32[]{:S(2)}) collective-permute-start(bf16[64,8,384]{2,1,0:T(8,128)(2,1)S(1)} %get-tuple-element.21), channel_id=1, source_target_pairs={{0,64},{32,96},{1,65},{33,97},{2,66},{34,98},{3,67},{35,99},{4,68}... | collective-permute-start | bytes 1179656 | tf_op jit(solution)/shard_map/ppermute | solution.py:30
  160.0 82.0 %collective-permute-start.19 = (bf16[64,8,384]{2,1,0:T(8,128)(2,1)S(1)}, bf16[64,8,384]{2,1,0:T(8,128)(2,1)}, u32[]{:S(2)}, u32[]{:S(2)}) collective-permute-start(bf16[64,8,384]{2,1,0:T(8,128)(2,1)S(1)} %get-tuple-element.21), channel_id=1, source_target_pairs={{0,16},{1,17},{2,18},{3,19},{4,20},{5,21},{6,22},{7,23},{8,24},{9,... | collective-permute-start | bytes 1179656 | tf_op jit(solution)/shard_map/ppermute | solution.py:30
  170.8 53.5 %collective-permute-start.21 = (bf16[64,8,384]{2,1,0:T(8,128)(2,1)S(1)}, bf16[64,8,384]{2,1,0:T(8,128)(2,1)}, u32[]{:S(2)}, u32[]{:S(2)}) collective-permute-start(bf16[64,8,384]{2,1,0:T(8,128)(2,1)S(1)} %get-tuple-element.21), channel_id=1, source_target_pairs={{64,0},{96,32},{65,1},{97,33},{66,2},{98,34},{67,3},{99,35},{68,4}... | collective-permute-start | bytes 1179656 | tf_op jit(solution)/shard_map/ppermute | solution.py:30
  174.3 18.1 %collective-permute-start.37 = (bf16[64,8,384]{2,1,0:T(8,128)(2,1)S(1)}, bf16[64,8,384]{2,1,0:T(8,128)(2,1)}, u32[]{:S(2)}, u32[]{:S(2)}) collective-permute-start(bf16[64,8,384]{2,1,0:T(8,128)(2,1)S(1)} %fusion.85), channel_id=1, source_target_pairs={{0,32},{32,64},{64,96},{1,33},{33,65},{65,97},{2,34},{34,66},{66,9... | collective-permute-start | bytes 1179656 | tf_op jit(solution)/shard_map/ppermute | solution.py:30
  180.1 19.0 %collective-permute-start.33 = (bf16[64,8,384]{2,1,0:T(8,128)(2,1)}, bf16[64,8,384]{2,1,0:T(8,128)(2,1)}, u32[]{:S(2)}, u32[]{:S(2)}) collective-permute-start(bf16[64,8,384]{2,1,0:T(8,128)(2,1)} %pad_maximum_fusion.16), channel_id=1, source_target_pairs={{4,0},{5,1},{6,2},{7,3},{8,4},{9,5},{10,6},{11,7},{12,8},{13,9},{1... | collective-permute-start | bytes 1179656 | tf_op jit(solution)/shard_map/ppermute | solution.py:30
  212.6 13.0 %collective-permute-start.39 = (bf16[64,8,384]{2,1,0:T(8,128)(2,1)S(1)}, bf16[64,8,384]{2,1,0:T(8,128)(2,1)S(1)}, u32[]{:S(2)}, u32[]{:S(2)}) collective-permute-start(bf16[64,8,384]{2,1,0:T(8,128)(2,1)S(1)} %pad_maximum_fusion.17), channel_id=1, source_target_pairs={{0,4},{1,5},{2,6},{3,7},{4,8},{5,9},{6,10},{7,11},{8,12},{9,13},{1... | collective-permute-start | bytes 1179656 | tf_op jit(solution)/shard_map/ppermute | solution.py:30
  217.1 34.0 %collective-permute-start.20 = (bf16[64,8,384]{2,1,0:T(8,128)(2,1)S(1)}, bf16[64,8,384]{2,1,0:T(8,128)(2,1)S(1)}, u32[]{:S(2)}, u32[]{:S(2)}) collective-permute-start(bf16[64,8,384]{2,1,0:T(8,128)(2,1)S(1)} %get-tuple-element.21), channel_id=1, source_target_pairs={{16,0},{17,1},{18,2},{19,3},{20,4},{21,5},{22,6},{23,7},{24,8},{25... | collective-permute-start | bytes 1179656 | tf_op jit(solution)/shard_map/ppermute | solution.py:30
  218.7 19.2 %collective-permute-start.17 = (bf16[64,8,384]{2,1,0:T(8,128)(2,1)}, bf16[64,8,384]{2,1,0:T(8,128)(2,1)S(1)}, u32[]{:S(2)}, u32[]{:S(2)}) collective-permute-start(bf16[64,8,384]{2,1,0:T(8,128)(2,1)} %collective-permute-done.16), channel_id=1, source_target_pairs={{0,16},{1,17},{2,18},{3,19},{4,20},{5,21},{6,22},{7,23},{8,24},{9,... | collective-permute-start | bytes 1179656 | tf_op jit(solution)/shard_map/ppermute | solution.py:30
  224.3 16.3 %collective-permute-start.18 = (bf16[64,8,384]{2,1,0:T(8,128)(2,1)}, bf16[64,8,384]{2,1,0:T(8,128)(2,1)S(1)}, u32[]{:S(2)}, u32[]{:S(2)}) collective-permute-start(bf16[64,8,384]{2,1,0:T(8,128)(2,1)} %collective-permute-done.16), channel_id=1, source_target_pairs={{16,0},{17,1},{18,2},{19,3},{20,4},{21,5},{22,6},{23,7},{24,8},{25... | collective-permute-start | bytes 1179656 | tf_op jit(solution)/shard_map/ppermute | solution.py:30
  225.6 25.6 %collective-permute-start.22 = (bf16[64,8,384]{2,1,0:T(8,128)(2,1)}, bf16[64,8,384]{2,1,0:T(8,128)(2,1)S(1)}, u32[]{:S(2)}, u32[]{:S(2)}) collective-permute-start(bf16[64,8,384]{2,1,0:T(8,128)(2,1)} %collective-permute-done.21), channel_id=1, source_target_pairs={{0,16},{1,17},{2,18},{3,19},{4,20},{5,21},{6,22},{7,23},{8,24},{9,... | collective-permute-start | bytes 1179656 | tf_op jit(solution)/shard_map/ppermute | solution.py:30
  237.9 14.6 %collective-permute-start.23 = (bf16[64,8,384]{2,1,0:T(8,128)(2,1)}, bf16[64,8,384]{2,1,0:T(8,128)(2,1)S(1)}, u32[]{:S(2)}, u32[]{:S(2)}) collective-permute-start(bf16[64,8,384]{2,1,0:T(8,128)(2,1)} %collective-permute-done.21), channel_id=1, source_target_pairs={{16,0},{17,1},{18,2},{19,3},{20,4},{21,5},{22,6},{23,7},{24,8},{25... | collective-permute-start | bytes 1179656 | tf_op jit(solution)/shard_map/ppermute | solution.py:30
  240.6 17.2 %collective-permute-start.41 = (bf16[4,8,384]{2,1,0:T(8,128)(2,1)S(1)}, bf16[4,8,384]{2,1,0:T(8,128)(2,1)S(1)}, u32[]{:S(2)}, u32[]{:S(2)}) collective-permute-start(bf16[4,8,384]{2,1,0:T(8,128)(2,1)S(1)} %get-tuple-element.41), channel_id=1, source_target_pairs={{32,0},{64,32},{96,64},{33,1},{65,33},{97,65},{34,2},{66,34},{98,6... | collective-permute-start | bytes 73736 | tf_op jit(solution)/shard_map/ppermute | solution.py:22
  242.0 15.8 %collective-permute-start.40 = (bf16[4,8,384]{2,1,0:T(8,128)(2,1)S(1)}, bf16[4,8,384]{2,1,0:T(8,128)(2,1)S(1)}, u32[]{:S(2)}, u32[]{:S(2)}) collective-permute-start(bf16[4,8,384]{2,1,0:T(8,128)(2,1)S(1)} %get-tuple-element.40), channel_id=1, source_target_pairs={{0,32},{32,64},{64,96},{1,33},{33,65},{65,97},{2,34},{34,66},{66,9... | collective-permute-start | bytes 73736 | tf_op jit(solution)/shard_map/ppermute | solution.py:19
  258.0 20.4 %collective-permute-start.43 = (bf16[72,4,384]{2,1,0:T(4,128)(2,1)S(1)}, bf16[72,4,384]{2,1,0:T(4,128)(2,1)S(1)}, u32[]{:S(2)}, u32[]{:S(2)}) collective-permute-start(bf16[72,4,384]{2,1,0:T(4,128)(2,1)S(1)} %get-tuple-element.24), channel_id=1, source_target_pairs={{0,1},{1,2},{2,3},{3,4},{4,5},{5,6},{6,7},{7,8},{8,9},{9,10},{10,1... | collective-permute-start | bytes 663560 | tf_op jit(solution)/shard_map/ppermute | solution.py:19
  259.3 19.0 %collective-permute-start.42 = (bf16[72,4,384]{2,1,0:T(4,128)(2,1)S(1)}, bf16[72,4,384]{2,1,0:T(4,128)(2,1)S(1)}, u32[]{:S(2)}, u32[]{:S(2)}) collective-permute-start(bf16[72,4,384]{2,1,0:T(4,128)(2,1)S(1)} %get-tuple-element.25), channel_id=1, source_target_pairs={{1,0},{2,1},{3,2},{4,3},{5,4},{6,5},{7,6},{8,7},{9,8},{10,9},{11,1... | collective-permute-start | bytes 663560 | tf_op jit(solution)/shard_map/ppermute | solution.py:22
  (70 other events, 1072.9 us)
Sparse Core Ops, SparseCore 0:
  296.5 234.5 all-reduce.6
where the time goes:
time: 552 us; the launch traced here: 543 us
  waiting for transfers between devices  241 us (44%)
  starting transfers between devices  164 us (30%)
  local copies, waits for them, and re-layouts  60.6 us (11%)
  matrix products  39.2 us (7%)
  other arithmetic  21.8 us (4%)
  between operations  16.6 us (3%)
    unnamed x2, waiting for transfers between devices  201 us
    ppermute x32, starting transfers between devices, passed_along(): return lax.ppermute(shard, axis, pairs)  115 us
    ppermute x8, starting transfers between devices, with_halo(): lax.ppermute(lax.slice_in_dim(block, block.shape[dim] - width, None, axis...  38 us
    ppermute x32, waiting for transfers between devices, passed_along(): return lax.ppermute(shard, axis, pairs)  34.5 us
    mul x4, local copies, waits for them, and re-layouts, backward_block(): local_term.reshape(-1) * scale  26.3 us
    unnamed x181, local copies, waits for them, and re-layouts  22.8 us
    dot_general x4, matrix products, backward_block(): lax.dot_general(patches, flat_grad, (((0,), (0,)), ((), ())), preferred_e...  17.7 us
    dot_general x4, matrix products, forward_block(): update = jnp.dot(patches, weight_block, preferred_element_type=jnp.float32)  11.1 us
  transfers between devices with their start and end apart: 49, of which 14 were waited for; matrix products, arithmetic and copies ran while one was open for 16% of the time, Pallas kernels for 0%

commit v1 on v0

v1 whole, which is shorter than its diff:
```python
import math

import jax
import jax.numpy as jnp
from jax import lax
from jax.experimental import pallas as pl
from jax.experimental.pallas import tpu as pltpu
from jax.sharding import PartitionSpec as P

F32 = jnp.float32
BF16 = jnp.bfloat16
MESH = pl.DeviceIdType.MESH
CH = 384
ROWS, COLS = 64, 8
CELLS = ROWS * COLS
TAPS = tuple((r, c) for r in (-1, 0, 1) for c in (-1, 0, 1))
EPSILON = 1e-05
ROOT = math.sqrt(2.0 / math.pi)
CUBIC = 0.044715
PITCH = 24
DIRS = ((0, -1), (0, 1), (-1, 0), (1, 0), (-1, -1), (-1, 1), (1, -1), (1, 1))
CHUNK = 27
ORDERS = (("x", "y", "z"), ("y", "z", "x"), ("z", "x", "y"))


def aligned(value, step):
    return value if isinstance(value, int) else pl.multiple_of(value, step)


def rows(start, size, step=16):
    return pl.ds(aligned(start, step), size)


def normed(stream):
    average = jnp.mean(stream, axis=-1, keepdims=True)
    centred = stream - average
    spread = jnp.mean(centred * centred, axis=-1, keepdims=True)
    inverse = lax.rsqrt(spread + EPSILON)
    return centred * inverse, inverse


def gelu(u):
    return 0.5 * u * (1.0 + jnp.tanh(ROOT * (u + CUBIC * (u * u * u))))


def gelu_slope(u):
    square = u * u
    t = jnp.tanh(ROOT * (u + CUBIC * (square * u)))
    return 0.5 * (1.0 + t) + 0.5 * u * (1.0 - t * t) * (ROOT * (1.0 + 3.0 * CUBIC * square))


def pulled(stream, gain, d_act):
    unit, inverse = normed(stream)
    d_unit = d_act * gelu_slope(unit * gain) * gain
    first = jnp.mean(d_unit, axis=-1, keepdims=True)
    second = jnp.mean(d_unit * unit, axis=-1, keepdims=True)
    return inverse * (d_unit - first - unit * second)


def strip_rows(d):
    return (ROWS * d, ROWS * d, max(COLS * d, 16), max(COLS * d, 16))


def kernel(
    x_ref, gains, w_hbm, cot, out, ig, wg_out,
    W, S, D, AT, F, V, U, G, SB, R0, L1, L2, L3, AS, AL, HS, HL,
    w_sem, hs_sem, hr_sem, as_sem, ar_sem, rs_sem, rr_sem,
):
    gx, gy = lax.axis_index("gx"), lax.axis_index("gy")
    core, y = gx % 2, (gx // 2) * 2 + gy // 16
    z, x = (gy // 4) % 4, gy % 4
    here = {"x": x, "y": y, "z": z}
    me = gx * 8 + gy // 4

    def device(core_of, at):
        return ((at["y"] // 2) * 2 + core_of, (at["y"] % 2) * 16 + at["z"] * 4 + at["x"])

    def plane(q):
        return (q // 8, (q % 8) * 4 + x)

    def exists(direction):
        r, c = gx + direction[0], gy + direction[1]
        return (r >= 0) & (r < 4) & (c >= 0) & (c < 32)

    barrier = pltpu.get_barrier_semaphore()

    def greet(target):
        pl.semaphore_signal(barrier, inc=1, device_id=target, device_id_type=MESH)

    @pl.loop(1, 32)
    def _(step):
        greet(plane((me + step) % 32))

    for step in (1, 2, 3):
        greet(device(core, {**here, "x": (x + step) % 4}))
    greeted = 34
    for direction in DIRS:
        there = exists(direction)

        @pl.when(there)
        def _(direction=direction):
            greet((gx + direction[0], gy + direction[1]))

        greeted = greeted + there.astype(jnp.int32)

    loads = []
    for k in range(4):
        loads.append(pltpu.make_async_copy(w_hbm.at[k], W.at[k], w_sem.at[k]))
        loads[k].start()

    def padded(at):
        return jnp.concatenate([F[p, at, :] for p in range(3)], axis=1)

    def pad_put(at, values):
        for p in range(3):
            F[p, at, :] = values[:, p * 128 : (p + 1) * 128]

    def halo_copy(slot, d, index):
        sizes = strip_rows(d)
        source = (0, 1, 2, 3, 2, 2, 3, 3)[index]
        size = sizes[source]
        starts = [sum(sizes[:i]) for i in range(4)]
        landed = (0, 1, 2, 3, 2, 2, 3, 3)
        lands = [sum(sizes[landed[j]] for j in range(i)) for i in range(8)]
        direction = DIRS[index]
        opposite = DIRS.index((-direction[0], -direction[1]))
        return pltpu.make_async_remote_copy(
            src_ref=HS.at[slot, pl.ds(starts[source], size)],
            dst_ref=HL.at[slot, pl.ds(lands[opposite], size)],
            send_sem=hs_sem.at[slot, index],
            recv_sem=hr_sem.at[slot, opposite],
            device_id=(gx + direction[0], gy + direction[1]),
            device_id_type=MESH,
        )

    def halo_send(slot, d):
        sizes = strip_rows(d)
        at = 0
        for first in (0, COLS - d):
            for j in range(d):
                column = padded(pl.ds(d * PITCH + 8 + first + j, ROWS, stride=PITCH))
                HS[slot, pl.ds(at + j * ROWS, ROWS), :] = column.astype(BF16)
            at += ROWS * d
        count = sizes[2] // COLS
        for first in (0, ROWS - count):
            for i in range(0, count, 2):
                pair = [padded(pl.ds((d + first + i + n) * PITCH + 8, 8)) for n in (0, 1)]
                HS[slot, pl.ds(at + i * 8, 16), :] = jnp.concatenate(pair, axis=0).astype(BF16)
            at += sizes[2]
        for index, direction in enumerate(DIRS):

            @pl.when(exists(direction))
            def _(index=index):
                halo_copy(slot, d, index).start()

    def halo_receive(slot, d):
        sizes = strip_rows(d)
        landed = (0, 1, 2, 3, 2, 2, 3, 3)
        lands = [sum(sizes[landed[j]] for j in range(i)) for i in range(8)]
        count = sizes[2] // COLS
        for index, direction in enumerate(DIRS):
            there = exists(direction)

            def put(values, index=index, direction=direction):
                if direction[0] == 0:
                    first = 8 - d if direction[1] < 0 else 16
                    for j in range(d):
                        pad_put(pl.ds(d * PITCH + first + j, ROWS, stride=PITCH), values(j * ROWS, ROWS))
                else:
                    first = 0 if direction[0] < 0 else d + ROWS
                    skip = count - d if direction[0] < 0 else 0
                    for i in range(0, count, 2):
                        both = values(i * 8, 16)
                        for n in (0, 1):
                            row = i + n - skip
                            if 0 <= row < d:
                                start = (first + row) * PITCH + 8 + 8 * direction[1]
                                pad_put(pl.ds(start, 8), both[n * 8 : n * 8 + 8])

            @pl.when(there)
            def _(index=index, direction=direction, put=put):
                opposite = DIRS.index((-direction[0], -direction[1]))
                halo_copy(slot, d, opposite).wait_recv()
                put(lambda at, size: HL[slot, pl.ds(lands[index] + at, size), :].astype(F32))

            @pl.when(jnp.logical_not(there))
            def _(put=put):
                put(lambda at, size: jnp.zeros((size, CH), F32))

    def near_versions(d):
        @pl.loop(0, (ROWS + 2 * d) // 2)
        def _(i):
            pair = [padded(rows((2 * i + n) * PITCH, PITCH, 8)) for n in (0, 1)]
            for c in (-1, 0, 1):
                both = [row[8 + c * d : 16 + c * d] for row in pair]
                V[c + 1, rows(i * 16, 16), :] = jnp.concatenate(both, axis=0).astype(BF16)

        if d == 1:

            @pl.loop(0, ROWS // 2)
            def _(i):
                pair = [padded(rows((2 * i + n + 1) * PITCH, PITCH, 8)) for n in (0, 1)]
                for c in (-1, 0, 1):
                    both = [row[8 + c * d : 16 + c * d] for row in pair]
                    U[c + 1, rows(i * 16, 16), :] = jnp.concatenate(both, axis=0).astype(BF16)

    def near_put(d, chunk, values):
        for i in range(8):
            pad_put(rows((d + chunk * 8 + i) * PITCH + 8, 8, 8), values[i * 8 : i * 8 + 8])

    def far_put(chunk, values):
        pad_put(rows(chunk * 128 + 32, 64, 8), values)

    def far_versions(s):
        for c in (-1, 0, 1):
            V[c + 1, pl.ds(0, s * 64), :] = jnp.zeros((s * 64, CH), BF16)
            V[c + 1, pl.ds((8 + s) * 64, s * 64), :] = jnp.zeros((s * 64, CH), BF16)

            @pl.loop(0, 8)
            def _(i, c=c):
                V[c + 1, rows((i + s) * 64, 64), :] = padded(rows(i * 128 + 32 + c * s * 8, 64, 8)).astype(BF16)

    def sources(step, sign):
        found = []
        for r, c in TAPS:
            r, c = sign * r, sign * c
            if step == 8 and r == 0:
                found.append((U.at[c + 1], 0))
            else:
                found.append((V.at[c + 1], (1 + r) * step))
        return found

    BLOCK = 256

    def convolve(k, step, sign, finish):
        found = sources(step, sign)

        @pl.loop(0, CELLS // BLOCK)
        def _(m):
            left = jnp.concatenate(
                [ref[rows(m * BLOCK + start, BLOCK), :] for ref, start in found], axis=1
            )
            if sign == 1:
                result = jnp.dot(left, W[k], preferred_element_type=F32)
            else:
                right = jnp.concatenate([W[k, t * CH : (t + 1) * CH, :] for t in range(9)], axis=1)
                result = lax.dot_general(left, right, (((1,), (1,)), ((), ())), preferred_element_type=F32)
            finish(rows(m * BLOCK, BLOCK), result)

    def act(k, slot, put):
        gain = gains[k : k + 1, :]

        @pl.loop(0, 8)
        def _(chunk):
            unit, _ = normed(S[slot, rows(chunk * 64, 64), :])
            acted = gelu(unit * gain).astype(BF16)
            D[rows(chunk * 64, 64), :] = acted.astype(F32)
            put(chunk, acted.astype(F32))

    def turn(k):
        AT[k] = D[...].T.astype(BF16)

    def kernel_gradient(k, step):
        found = sources(step, -1)
        for first in (0, 2, 4, 6, 8):
            pair = found[first : first + 2]
            right = jnp.concatenate([ref[pl.ds(start, CELLS), :] for ref, start in pair], axis=1)
            both = jnp.dot(AT[k], right, preferred_element_type=F32)
            for n in range(len(pair)):
                G[pl.ds((first + n) * CH, CH), :] = both[:, n * CH : (n + 1) * CH]

    def plane_send(slot):
        @pl.loop(1, 32)
        def _(step):
            q = (me + step) % 32
            pltpu.make_async_remote_copy(
                src_ref=AS.at[slot, rows(q * 16, 16)],
                dst_ref=AL.at[slot, rows(me * 16, 16)],
                send_sem=as_sem.at[slot],
                recv_sem=ar_sem.at[slot],
                device_id=plane(q),
                device_id_type=MESH,
            ).start()

        AL[slot, rows(me * 16, 16), :] = AS[slot, rows(me * 16, 16), :]

    def plane_wait(slot, sem):
        part = AL.at[slot, pl.ds(0, 31 * 16)]
        pltpu.make_async_copy(part, part, sem.at[slot]).wait()

    def to_far(slot, load):
        @pl.loop(0, 32)
        def _(q):
            both = jnp.concatenate([load(rows(q * 8, 8, 8)), load(rows(q * 8 + 256, 8, 8))], axis=0)
            AS[slot, rows(q * 16, 16), :] = both.astype(BF16)

        plane_send(slot)

    def at_far(slot, store):
        plane_wait(slot, ar_sem)

        @pl.loop(0, 32)
        def _(q):
            both = AL[slot, rows(q * 16, 16), :].astype(F32)
            base = ((q // 8) * 16 + q % 8) * 8
            store(rows(base, 8, 8), both[0:8])
            store(rows(base + 64, 8, 8), both[8:16])

    def to_near(slot, load):
        @pl.loop(0, 32)
        def _(q):
            base = ((q // 8) * 16 + q % 8) * 8
            both = jnp.concatenate([load(rows(base, 8, 8)), load(rows(base + 64, 8, 8))], axis=0)
            AS[slot, rows(q * 16, 16), :] = both.astype(BF16)

        plane_send(slot)

    def at_near(slot, store):
        plane_wait(slot, ar_sem)

        @pl.loop(0, 32)
        def _(q):
            both = AL[slot, rows(q * 16, 16), :].astype(F32)
            store(rows(q * 8, 8, 8), both[0:8])
            store(rows(q * 8 + 256, 8, 8), both[8:16])

    def sibling_copy(k, p):
        return pltpu.make_async_remote_copy(
            src_ref=SB.at[k % 2, p, rows((1 - core) * 2048, 2048)],
            dst_ref=R0.at[k, p],
            send_sem=rs_sem.at[k, p, 0],
            recv_sem=rr_sem.at[k, p, 0],
            device_id=(gx + 1 - 2 * core, gy),
            device_id_type=MESH,
        )

    def held(p, level):
        base, size = core * 64, 64
        for n in range(level):
            size = size // 4
            base = base + here[ORDERS[p][n]] * size
        return base, size

    def axis_copy(k, p, level, step):
        axis = ORDERS[p][level - 1]
        base, size = held(p, level - 1)
        size = size // 4
        to = (here[axis] + step) % 4
        land = (None, L1, L2, L3)[level]
        return pltpu.make_async_remote_copy(
            src_ref=SB.at[k % 2, p, rows((base + to * size) * 32, size * 32)],
            dst_ref=land.at[k, p, step - 1],
            send_sem=rs_sem.at[k, p, level * 3 - 3 + step],
            recv_sem=rr_sem.at[k, p, level * 3 - 3 + step],
            device_id=device(core, {**here, axis: to}),
            device_id_type=MESH,
        )

    def reduce_0(k):
        if k < 2:
            reduce_sent(k + 2)

        @pl.loop(0, 16)
        def _(group):
            for n in range(8):
                chunk = group * 8 + n
                at = {"x": n % 4, "z": (chunk // 4) % 4, "y": (chunk // 64) * 2 + (chunk // 16) % 2}
                skip = CHUNK * n % 8
                values = G[rows(group * 8 * CHUNK + CHUNK * n - skip, 40, 8), :][skip : skip + 32]
                for p in range(3):
                    a, b, c = (at[axis] for axis in ORDERS[p])
                    to = ((chunk // 32) % 2) * 64 + a * 16 + b * 4 + c
                    SB[k % 2, p, rows(to * 32, 32), :] = values[:, p * 128 : (p + 1) * 128].astype(BF16)

        for p in range(3):
            sibling_copy(k, p).start()

    def reduce_sent(k):
        for p in range(3):
            sibling_copy(k, p).wait_send()
            for level in (1, 2, 3):
                for step in (1, 2, 3):
                    axis_copy(k, p, level, step).wait_send()

    def reduce_1(k):
        for p in range(3):
            sibling_copy(k, p).wait_recv()

            @pl.loop(0, 8)
            def _(i, p=p):
                own = rows(core * 2048 + i * 256, 256)
                total = SB[k % 2, p, own, :].astype(F32) + R0[k, p, rows(i * 256, 256), :].astype(F32)
                SB[k % 2, p, own, :] = total.astype(BF16)

            for step in (2, 1, 3):
                axis_copy(k, p, 1, step).start()

    def gathered(k, p, level, part, start):
        land = (None, L1, L2, L3)[level]
        base, _ = held(p, level)
        total = SB[k % 2, p, rows(base * 32 + start, part), :].astype(F32)
        for step in (1, 2, 3):
            total = total + land[k, p, step - 1, rows(start, part), :].astype(F32)
        return total

    def reduce_next(k, level):
        for p in range(3):
            for step in (1, 2, 3):
                axis_copy(k, p, level, step).wait_recv()
            base, size = held(p, level)
            part = 128

            @pl.loop(0, size * 32 // part)
            def _(i, p=p, base=base):
                total = gathered(k, p, level, part, i * part)
                SB[k % 2, p, rows(base * 32 + i * part, part), :] = total.astype(BF16)

            for step in (2, 1, 3):
                axis_copy(k, p, level + 1, step).start()

    def reduce_last(k):
        for p in range(3):
            for step in (1, 2, 3):
                axis_copy(k, p, 3, step).wait_recv()
            wg_out[k, :, p * 128 : (p + 1) * 128] = gathered(k, p, 3, 32, 0) * (1.0 / 256.0)

    @pl.loop(0, 8)
    def _(chunk):
        S[0, rows(chunk * 64, 64), :] = x_ref[rows(chunk * 64, 64), :].astype(F32)

    act(0, 0, lambda chunk, values: near_put(1, chunk, values))
    pl.semaphore_wait(barrier, greeted)
    halo_send(0, 1)
    to_far(0, lambda at: cot[at, :])
    turn(0)
    loads[0].wait()
    halo_receive(0, 1)
    near_versions(1)

    def grow(slot):
        def finish(at, result):
            S[slot + 1, at, :] = S[slot, at, :] + result

        return finish

    convolve(0, 8, 1, grow(0))

    act(1, 1, lambda chunk, values: near_put(4, chunk, values))
    halo_send(1, 4)
    turn(1)
    loads[1].wait()
    halo_receive(1, 4)
    near_versions(4)
    convolve(1, 32, 1, grow(1))

    to_far(1, lambda at: S[2, at, :])
    loads[2].wait()
    loads[3].wait()

    @pl.loop(0, 8)
    def _(i):
        pad_put(rows(i * 128, 32, 8), jnp.zeros((32, CH), F32))
        pad_put(rows(i * 128 + 96, 32, 8), jnp.zeros((32, CH), F32))

    def store_stream(at, values):
        S[3, at, :] = values

    at_far(1, store_stream)

    act(2, 3, far_put)
    far_versions(1)
    convolve(2, 64, 1, grow(3))
    turn(2)
    act(3, 4, far_put)
    far_versions(4)

    def keep_updates(at, result):
        S[5, at, :] = (S[4, at, :] - S[3, at, :]) + result

    convolve(3, 256, 1, keep_updates)
    to_near(2, lambda at: S[5, at, :])
    turn(3)

    def store_gradient(at, values):
        S[6, at, :] = values

    at_far(0, store_gradient)

    def put_gradient(slot, put):
        @pl.loop(0, 8)
        def _(chunk):
            put(chunk, S[slot, rows(chunk * 64, 64), :].astype(BF16).astype(F32))

    def keep_d_act(at, result):
        D[at, :] = result

    def pull(k, stream_slot, finish):
        gain = gains[k : k + 1, :]

        @pl.loop(0, 8)
        def _(chunk):
            at = rows(chunk * 64, 64)
            finish(chunk, at, pulled(S[stream_slot, at, :], gain, D[at, :]))

    put_gradient(6, far_put)
    far_versions(4)
    kernel_gradient(3, 256)
    reduce_0(3)
    convolve(3, 256, -1, keep_d_act)

    def far_3(chunk, at, pulled_back):
        S[5, at, :] = pulled_back
        S[6, at, :] = S[6, at, :] + pulled_back

    pull(3, 4, far_3)
    put_gradient(6, far_put)
    far_versions(1)
    reduce_1(3)
    convolve(2, 64, -1, keep_d_act)

    def far_2(chunk, at, pulled_back):
        S[5, at, :] = S[5, at, :] + pulled_back

    pull(2, 3, far_2)
    to_near(3, lambda at: S[5, at, :])
    reduce_next(3, 1)
    kernel_gradient(2, 64)
    reduce_0(2)

    def store_output(at, values):
        out[at, :] = S[2, at, :] + values

    at_near(2, store_output)

    def store_near_gradient(at, values):
        S[6, at, :] = cot[at, :] + values

    at_near(3, store_near_gradient)
    put_gradient(6, lambda chunk, values: near_put(4, chunk, values))
    halo_send(2, 4)
    reduce_next(3, 2)
    reduce_1(2)
    halo_receive(2, 4)
    near_versions(4)
    convolve(1, 32, -1, keep_d_act)

    def near_1(chunk, at, pulled_back):
        total = S[6, at, :] + pulled_back
        S[6, at, :] = total
        near_put(1, chunk, total.astype(BF16).astype(F32))

    pull(1, 1, near_1)
    halo_send(3, 1)
    reduce_last(3)
    reduce_next(2, 1)
    kernel_gradient(1, 32)
    reduce_0(1)
    halo_receive(3, 1)
    near_versions(1)
    kernel_gradient(0, 8)
    reduce_next(2, 2)
    reduce_1(1)
    reduce_last(2)
    reduce_0(0)
    convolve(0, 8, -1, keep_d_act)

    def near_0(chunk, at, pulled_back):
        ig[at, :] = S[6, at, :] + pulled_back

    reduce_next(1, 1)
    pull(0, 0, near_0)
    reduce_1(0)
    reduce_next(1, 2)
    reduce_next(0, 1)
    reduce_last(1)
    reduce_next(0, 2)
    reduce_last(0)

    reduce_sent(1)
    reduce_sent(0)
    for slot in range(4):
        plane_wait(slot, as_sem)
    for slot, d in enumerate((1, 4, 4, 1)):
        for index, direction in enumerate(DIRS):

            @pl.when(exists(direction))
            def _(slot=slot, d=d, index=index):
                halo_copy(slot, d, index).wait_send()


def body(inputs, norm_gains, weights, cotangent):
    vmem = pl.BlockSpec(memory_space=pltpu.VMEM)
    out, input_grad, shares = pl.pallas_call(
        kernel,
        out_shape=(
            jax.ShapeDtypeStruct((CELLS, CH), F32),
            jax.ShapeDtypeStruct((CELLS, CH), F32),
            jax.ShapeDtypeStruct((4, 32, CH), F32),
        ),
        in_specs=[vmem, vmem, pl.BlockSpec(memory_space=pl.ANY), vmem],
        out_specs=(vmem, vmem, vmem),
        scratch_shapes=[
            pltpu.VMEM((4, 9 * CH, CH), BF16),
            pltpu.VMEM((7, CELLS, CH), F32),
            pltpu.VMEM((CELLS, CH), F32),
            pltpu.VMEM((4, CH, CELLS), BF16),
            pltpu.VMEM((3, 72 * PITCH, 128), F32),
            pltpu.VMEM((3, 1024, CH), BF16),
            pltpu.VMEM((3, CELLS, CH), BF16),
            pltpu.VMEM((9 * CH + 16, CH), F32),
            pltpu.VMEM((2, 3, 4096, 128), BF16),
            pltpu.VMEM((4, 3, 2048, 128), BF16),
            pltpu.VMEM((4, 3, 3, 512, 128), BF16),
            pltpu.VMEM((4, 3, 3, 128, 128), BF16),
            pltpu.VMEM((4, 3, 3, 32, 128), BF16),
            pltpu.VMEM((4, CELLS, CH), BF16),
            pltpu.VMEM((4, CELLS, CH), BF16),
            pltpu.VMEM((4, 576, CH), BF16),
            pltpu.VMEM((4, 704, CH), BF16),
            pltpu.SemaphoreType.DMA((4,)),
            pltpu.SemaphoreType.DMA((4, 8)),
            pltpu.SemaphoreType.DMA((4, 8)),
            pltpu.SemaphoreType.DMA((4,)),
            pltpu.SemaphoreType.DMA((4,)),
            pltpu.SemaphoreType.DMA((4, 3, 10)),
            pltpu.SemaphoreType.DMA((4, 3, 10)),
        ],
        compiler_params=pltpu.CompilerParams(
            collective_id=0, has_side_effects=True, vmem_limit_bytes=64 * 1024 * 1024
        ),
        cost_estimate=pl.CostEstimate(flops=16_300_000_000, bytes_accessed=15_000_000, transcendentals=4_000_000),
    )(inputs.reshape(CELLS, CH), norm_gains, weights, cotangent.reshape(CELLS, CH))
    shape = (ROWS, COLS, CH)
    return (
        out.reshape(shape),
        input_grad.reshape(shape),
        shares[:, :CHUNK].reshape(4, CHUNK * CH),
    )


def solution(mesh):
    placed = (P("gx", "gy", None), P(), P(), P("gx", "gy", None))
    return jax.shard_map(
        body,
        mesh=mesh,
        in_specs=placed,
        out_specs=(P("gx", "gy", None), P("gx", "gy", None), P(None, ("gx", "gy"))),
        check_vma=False,
    )
```

time: 552 us -> 144 us (0.26); the launches traced: 543 us -> 144 us
  waiting for transfers between devices: 241 us -> 0 us
  starting transfers between devices: 164 us -> 0 us
  Pallas kernels: 0 us -> 138 us
  local copies, waits for them, and re-layouts: 60.6 us -> 5.84 us
  matrix products: 39.2 us -> 0 us
  other arithmetic: 21.8 us -> 0 us
  between operations: 16.6 us -> 0.64 us
    unnamed x2 -> x0, waiting for transfers between devices: 201 us -> none
    ppermute x48 -> x0, starting transfers between devices: 164 us -> none  [the longest x32 115 us: passed_along(): return lax.ppermute(shard, axis, pairs)]
    pallas_call x0 -> x1, Pallas kernels: none -> 138 us  [body(): pl.pallas_call(kernel, out_shape=(jax.ShapeDtypeStruct((CELLS, CH), F32),...]
    ppermute x48 -> x0, waiting for transfers between devices: 39.2 us -> none  [the longest x32 34.5 us: passed_along(): return lax.ppermute(shard, axis, pairs)]
    dot_general x12 -> x0, matrix products: 39.2 us -> none  [the longest x4 17.7 us: backward_block(): lax.dot_general(patches, flat_grad, (((0,), (0,)), ((), ())), preferred_e...]
    mul x4 -> x0, local copies, waits for them, and re-layouts: 26.3 us -> none  [backward_block(): local_term.reshape(-1) * scale]
    unnamed x181 -> x4, local copies, waits for them, and re-layouts: 22.8 us -> 5.84 us
    slice x14 -> x0, local copies, waits for them, and re-layouts: 10.2 us -> none  [the longest x1 7.2 us: body(): weights[block_index]]
  transfers between devices with their start and end apart: 49 -> 0, of which waited for: 14 -> 0; matrix products, arithmetic and copies ran while one was open for 16% -> 0% of each run, Pallas kernels for 0% -> 0%
where the time goes in v1:
time: 144 us
  Pallas kernels  138 us (96%)
  local copies, waits for them, and re-layouts  5.84 us (4%)
    pallas_call x1, Pallas kernels, body(): pl.pallas_call(kernel, out_shape=(jax.ShapeDtypeStruct((CELLS, CH), F32),...  138 us
    unnamed x4, local copies, waits for them, and re-layouts  5.84 us

profile of v1, /device:TPU:0, one launch (start us, length us, event | category | flops | bytes accessed | tf_op | source)
XLA Modules:
  0.0 144.2 jit_solution(8195818375026897331)
XLA Ops:
  0.6 137.7 %shard_map.67 = (f32[512,384]{1,0:T(8,128)}, f32[512,384]{1,0:T(8,128)}, f32[4,32,384]{2,1,0:T(8,128)}) custom-call(bf16[512,384]{1,0:T(8,128)(2,1)} %bitcast.11, f32[4,384]{1,0:T(4,128)} %gains.1, bf16[4,3456,384]{2,1,0:T(8,128)(2,1)} %w_hbm.1, f32[512,384]{1,0:T(8,128)} %bitcast.10), custom_call_target="tpu_custom_call" | custom-call | flops 16300000256 | bytes 15000000 | tf_op jit(solution)/shard_map/pallas_call | solution.py:593
  138.4 0.9 slice_bitcast_fusion
  139.3 0.8 copy.7
  140.1 2.1 %copy.10 = f32[64,8,384]{2,1,0:T(8,128)} copy(f32[64,8,384]{2,1,0:T(8,128)} %bitcast.8) | data formatting | bytes 1572864
  142.2 2.1 %copy.11 = f32[64,8,384]{2,1,0:T(8,128)} copy(f32[64,8,384]{2,1,0:T(8,128)} %bitcast.7) | data formatting | bytes 1572864

commit v2 on v1

--- a/solution.py
+++ b/solution.py
@@ -40,17 +40,18 @@
 
 
 def gelu(u):
-    return 0.5 * u * (1.0 + jnp.tanh(ROOT * (u + CUBIC * (u * u * u))))
+    half = 0.5 * u
+    return half + half * jnp.tanh(u * (ROOT + (ROOT * CUBIC) * (u * u)))
 
 
 def gelu_slope(u):
     square = u * u
-    t = jnp.tanh(ROOT * (u + CUBIC * (square * u)))
-    return 0.5 * (1.0 + t) + 0.5 * u * (1.0 - t * t) * (ROOT * (1.0 + 3.0 * CUBIC * square))
-
-
-def pulled(stream, gain, d_act):
-    unit, inverse = normed(stream)
+    t = jnp.tanh(u * (ROOT + (ROOT * CUBIC) * square))
+    rest = (1.0 - t) * u * (ROOT + (3.0 * ROOT * CUBIC) * square)
+    return (0.5 + 0.5 * t) * (1.0 + rest)
+
+
+def pulled(unit, inverse, gain, d_act):
     d_unit = d_act * gelu_slope(unit * gain) * gain
     first = jnp.mean(d_unit, axis=-1, keepdims=True)
     second = jnp.mean(d_unit * unit, axis=-1, keepdims=True)
@@ -62,21 +63,21 @@
 
 
 def kernel(
-    x_ref, gains, w_hbm, cot, out, ig, wg_out,
-    W, S, D, AT, F, V, U, G, SB, R0, L1, L2, L3, AS, AL, HS, HL,
-    w_sem, hs_sem, hr_sem, as_sem, ar_sem, rs_sem, rr_sem,
+    x_hbm, gains, w_hbm, cot_hbm, out, ig, wg_out,
+    W, X, CT, S, D, UN, IV, AT, F, V, U, G, SB, R0, L1, L2, L3, AS, AL, HS, HL,
+    w_sem, io_sem, hs_sem, hr_sem, as_sem, ar_sem, rs_sem, rr_sem,
 ):
     gx, gy = lax.axis_index("gx"), lax.axis_index("gy")
-    core, y = gx % 2, (gx // 2) * 2 + gy // 16
-    z, x = (gy // 4) % 4, gy % 4
+    core, y = gx & 1, (gx >> 1) * 2 + (gy >> 4)
+    z, x = (gy >> 2) & 3, gy & 3
     here = {"x": x, "y": y, "z": z}
-    me = gx * 8 + gy // 4
+    me = gx * 8 + (gy >> 2)
 
     def device(core_of, at):
-        return ((at["y"] // 2) * 2 + core_of, (at["y"] % 2) * 16 + at["z"] * 4 + at["x"])
+        return ((at["y"] >> 1) * 2 + core_of, (at["y"] & 1) * 16 + at["z"] * 4 + at["x"])
 
     def plane(q):
-        return (q // 8, (q % 8) * 4 + x)
+        return (q >> 3, (q & 7) * 4 + x)
 
     def exists(direction):
         r, c = gx + direction[0], gy + direction[1]
@@ -89,10 +90,10 @@
 
     @pl.loop(1, 32)
     def _(step):
-        greet(plane((me + step) % 32))
+        greet(plane((me + step) & 31))
 
     for step in (1, 2, 3):
-        greet(device(core, {**here, "x": (x + step) % 4}))
+        greet(device(core, {**here, "x": (x + step) & 3}))
     greeted = 34
     for direction in DIRS:
         there = exists(direction)
@@ -103,6 +104,10 @@
 
         greeted = greeted + there.astype(jnp.int32)
 
+    load_x = pltpu.make_async_copy(x_hbm, X, io_sem.at[0])
+    load_x.start()
+    load_cot = pltpu.make_async_copy(cot_hbm, CT, io_sem.at[1])
+    load_cot.start()
     loads = []
     for k in range(4):
         loads.append(pltpu.make_async_copy(w_hbm.at[k], W.at[k], w_sem.at[k]))
@@ -153,6 +158,13 @@
             def _(index=index):
                 halo_copy(slot, d, index).start()
 
+    def halo_sent(slot, d):
+        for index, direction in enumerate(DIRS):
+
+            @pl.when(exists(direction))
+            def _(index=index):
+                halo_copy(slot, d, index).wait_send()
+
     def halo_receive(slot, d):
         sizes = strip_rows(d)
         landed = (0, 1, 2, 3, 2, 2, 3, 3)
@@ -252,7 +264,9 @@
 
         @pl.loop(0, 8)
         def _(chunk):
-            unit, _ = normed(S[slot, rows(chunk * 64, 64), :])
+            unit, inverse = normed(S[slot, rows(chunk * 64, 64), :])
+            UN[k, rows(chunk * 64, 64), :] = unit
+            IV[k, rows(chunk * 64, 64), :] = jnp.broadcast_to(inverse, (64, 128))
             acted = gelu(unit * gain).astype(BF16)
             D[rows(chunk * 64, 64), :] = acted.astype(F32)
             put(chunk, acted.astype(F32))
@@ -267,12 +281,13 @@
             right = jnp.concatenate([ref[pl.ds(start, CELLS), :] for ref, start in pair], axis=1)
             both = jnp.dot(AT[k], right, preferred_element_type=F32)
             for n in range(len(pair)):
-                G[pl.ds((first + n) * CH, CH), :] = both[:, n * CH : (n + 1) * CH]
+                for p in range(3):
+                    G[p, pl.ds((first + n) * CH, CH), :] = both[:, n * CH + p * 128 : n * CH + (p + 1) * 128]
 
     def plane_send(slot):
         @pl.loop(1, 32)
         def _(step):
-            q = (me + step) % 32
+            q = (me + step) & 31
             pltpu.make_async_remote_copy(
                 src_ref=AS.at[slot, rows(q * 16, 16)],
                 dst_ref=AL.at[slot, rows(me * 16, 16)],
@@ -288,6 +303,9 @@
         part = AL.at[slot, pl.ds(0, 31 * 16)]
         pltpu.make_async_copy(part, part, sem.at[slot]).wait()
 
+    def plane_sent(slot):
+        plane_wait(slot, as_sem)
+
     def to_far(slot, load):
         @pl.loop(0, 32)
         def _(q):
@@ -302,14 +320,14 @@
         @pl.loop(0, 32)
         def _(q):
             both = AL[slot, rows(q * 16, 16), :].astype(F32)
-            base = ((q // 8) * 16 + q % 8) * 8
+            base = ((q >> 3) * 16 + (q & 7)) * 8
             store(rows(base, 8, 8), both[0:8])
             store(rows(base + 64, 8, 8), both[8:16])
 
     def to_near(slot, load):
         @pl.loop(0, 32)
         def _(q):
-            base = ((q // 8) * 16 + q % 8) * 8
+            base = ((q >> 3) * 16 + (q & 7)) * 8
             both = jnp.concatenate([load(rows(base, 8, 8)), load(rows(base + 64, 8, 8))], axis=0)
             AS[slot, rows(q * 16, 16), :] = both.astype(BF16)
 
@@ -345,7 +363,7 @@
         axis = ORDERS[p][level - 1]
         base, size = held(p, level - 1)
         size = size // 4
-        to = (here[axis] + step) % 4
+        to = (here[axis] + step) & 3
         land = (None, L1, L2, L3)[level]
         return pltpu.make_async_remote_copy(
             src_ref=SB.at[k % 2, p, rows((base + to * size) * 32, size * 32)],
@@ -360,17 +378,22 @@
         if k < 2:
             reduce_sent(k + 2)
 
-        @pl.loop(0, 16)
-        def _(group):
-            for n in range(8):
-                chunk = group * 8 + n
-                at = {"x": n % 4, "z": (chunk // 4) % 4, "y": (chunk // 64) * 2 + (chunk // 16) % 2}
-                skip = CHUNK * n % 8
-                values = G[rows(group * 8 * CHUNK + CHUNK * n - skip, 40, 8), :][skip : skip + 32]
-                for p in range(3):
-                    a, b, c = (at[axis] for axis in ORDERS[p])
-                    to = ((chunk // 32) % 2) * 64 + a * 16 + b * 4 + c
-                    SB[k % 2, p, rows(to * 32, 32), :] = values[:, p * 128 : (p + 1) * 128].astype(BF16)
+        @pl.loop(0, 2)
+        def _(high):
+            @pl.loop(0, 2)
+            def _(half):
+                @pl.loop(0, 2)
+                def _(low):
+                    @pl.loop(0, 2)
+                    def _(pair):
+                        first = (high * 4 + half * 2 + low) * 16 + pair * 8
+                        for p in range(3):
+                            eight = G.at[p, rows(first * CHUNK, 8 * CHUNK + 8, 8)]
+                            for n in range(8):
+                                at = {"x": n % 4, "z": pair * 2 + n // 4, "y": high * 2 + low}
+                                a, b, c = (at[axis] for axis in ORDERS[p])
+                                to = half * 64 + a * 16 + b * 4 + c
+                                SB[k % 2, p, rows(to * 32, 32), :] = eight[pl.ds(CHUNK * n, 32), :].astype(BF16)
 
         for p in range(3):
             sibling_copy(k, p).start()
@@ -386,11 +409,10 @@
         for p in range(3):
             sibling_copy(k, p).wait_recv()
 
-            @pl.loop(0, 8)
+            @pl.loop(0, 4)
             def _(i, p=p):
-                own = rows(core * 2048 + i * 256, 256)
-                total = SB[k % 2, p, own, :].astype(F32) + R0[k, p, rows(i * 256, 256), :].astype(F32)
-                SB[k % 2, p, own, :] = total.astype(BF16)
+                own = rows(core * 2048 + i * 512, 512)
+                SB[k % 2, p, own, :] = SB[k % 2, p, own, :] + R0[k, p, rows(i * 512, 512), :]
 
             for step in (2, 1, 3):
                 axis_copy(k, p, 1, step).start()
@@ -408,7 +430,7 @@
             for step in (1, 2, 3):
                 axis_copy(k, p, level, step).wait_recv()
             base, size = held(p, level)
-            part = 128
+            part = min(256, size * 32)
 
             @pl.loop(0, size * 32 // part)
             def _(i, p=p, base=base):
@@ -422,16 +444,21 @@
         for p in range(3):
             for step in (1, 2, 3):
                 axis_copy(k, p, 3, step).wait_recv()
-            wg_out[k, :, p * 128 : (p + 1) * 128] = gathered(k, p, 3, 32, 0) * (1.0 / 256.0)
+            total = gathered(k, p, 3, 32, 0) * (1.0 / 256.0)
+            for r in range(CHUNK):
+                wg_out[k : k + 1, r * CH + p * 128 : r * CH + (p + 1) * 128] = total[r : r + 1]
+
+    load_x.wait()
 
     @pl.loop(0, 8)
     def _(chunk):
-        S[0, rows(chunk * 64, 64), :] = x_ref[rows(chunk * 64, 64), :].astype(F32)
+        S[0, rows(chunk * 64, 64), :] = X[rows(chunk * 64, 64), :].astype(F32)
 
     act(0, 0, lambda chunk, values: near_put(1, chunk, values))
     pl.semaphore_wait(barrier, greeted)
     halo_send(0, 1)
-    to_far(0, lambda at: cot[at, :])
+    load_cot.wait()
+    to_far(0, lambda at: CT[at, :])
     turn(0)
     loads[0].wait()
     halo_receive(0, 1)
@@ -494,13 +521,13 @@
     def keep_d_act(at, result):
         D[at, :] = result
 
-    def pull(k, stream_slot, finish):
+    def pull(k, finish):
         gain = gains[k : k + 1, :]
 
         @pl.loop(0, 8)
         def _(chunk):
             at = rows(chunk * 64, 64)
-            finish(chunk, at, pulled(S[stream_slot, at, :], gain, D[at, :]))
+            finish(chunk, at, pulled(UN[k, at, :], IV[k, at, :][:, :1], gain, D[at, :]))
 
     put_gradient(6, far_put)
     far_versions(4)
@@ -512,7 +539,7 @@
         S[5, at, :] = pulled_back
         S[6, at, :] = S[6, at, :] + pulled_back
 
-    pull(3, 4, far_3)
+    pull(3, far_3)
     put_gradient(6, far_put)
     far_versions(1)
     reduce_1(3)
@@ -521,19 +548,22 @@
     def far_2(chunk, at, pulled_back):
         S[5, at, :] = S[5, at, :] + pulled_back
 
-    pull(2, 3, far_2)
+    pull(2, far_2)
     to_near(3, lambda at: S[5, at, :])
     reduce_next(3, 1)
     kernel_gradient(2, 64)
     reduce_0(2)
 
     def store_output(at, values):
-        out[at, :] = S[2, at, :] + values
+        S[2, at, :] = (S[2, at, :] - S[0, at, :]) + values
 
     at_near(2, store_output)
+    save_out = pltpu.make_async_copy(S.at[2], out, io_sem.at[2])
+    save_out.start()
 
     def store_near_gradient(at, values):
-        S[6, at, :] = cot[at, :] + values
+        S[6, at, :] = CT[at, :] + values
+        S[5, at, :] = values
 
     at_near(3, store_near_gradient)
     put_gradient(6, lambda chunk, values: near_put(4, chunk, values))
@@ -546,10 +576,10 @@
 
     def near_1(chunk, at, pulled_back):
         total = S[6, at, :] + pulled_back
-        S[6, at, :] = total
+        S[5, at, :] = S[5, at, :] + pulled_back
         near_put(1, chunk, total.astype(BF16).astype(F32))
 
-    pull(1, 1, near_1)
+    pull(1, near_1)
     halo_send(3, 1)
     reduce_last(3)
     reduce_next(2, 1)
@@ -565,10 +595,12 @@
     convolve(0, 8, -1, keep_d_act)
 
     def near_0(chunk, at, pulled_back):
-        ig[at, :] = S[6, at, :] + pulled_back
+        S[5, at, :] = S[5, at, :] + pulled_back
 
     reduce_next(1, 1)
-    pull(0, 0, near_0)
+    pull(0, near_0)
+    save_ig = pltpu.make_async_copy(S.at[5], ig, io_sem.at[3])
+    save_ig.start()
     reduce_1(0)
     reduce_next(1, 2)
     reduce_next(0, 1)
@@ -576,38 +608,42 @@
     reduce_next(0, 2)
     reduce_last(0)
 
+    save_out.wait()
+    save_ig.wait()
+
     reduce_sent(1)
     reduce_sent(0)
     for slot in range(4):
-        plane_wait(slot, as_sem)
+        plane_sent(slot)
     for slot, d in enumerate((1, 4, 4, 1)):
-        for index, direction in enumerate(DIRS):
-
-            @pl.when(exists(direction))
-            def _(slot=slot, d=d, index=index):
-                halo_copy(slot, d, index).wait_send()
+        halo_sent(slot, d)
 
 
 def body(inputs, norm_gains, weights, cotangent):
     vmem = pl.BlockSpec(memory_space=pltpu.VMEM)
+    hbm = pl.BlockSpec(memory_space=pl.ANY)
     out, input_grad, shares = pl.pallas_call(
         kernel,
         out_shape=(
             jax.ShapeDtypeStruct((CELLS, CH), F32),
             jax.ShapeDtypeStruct((CELLS, CH), F32),
-            jax.ShapeDtypeStruct((4, 32, CH), F32),
+            jax.ShapeDtypeStruct((4, CHUNK * CH), F32),
         ),
-        in_specs=[vmem, vmem, pl.BlockSpec(memory_space=pl.ANY), vmem],
-        out_specs=(vmem, vmem, vmem),
+        in_specs=[hbm, vmem, hbm, hbm],
+        out_specs=(hbm, hbm, vmem),
         scratch_shapes=[
             pltpu.VMEM((4, 9 * CH, CH), BF16),
+            pltpu.VMEM((CELLS, CH), BF16),
+            pltpu.VMEM((CELLS, CH), F32),
             pltpu.VMEM((7, CELLS, CH), F32),
             pltpu.VMEM((CELLS, CH), F32),
+            pltpu.VMEM((4, CELLS, CH), F32),
+            pltpu.VMEM((4, CELLS, 128), F32),
             pltpu.VMEM((4, CH, CELLS), BF16),
             pltpu.VMEM((3, 72 * PITCH, 128), F32),
             pltpu.VMEM((3, 1024, CH), BF16),
             pltpu.VMEM((3, CELLS, CH), BF16),
-            pltpu.VMEM((9 * CH + 16, CH), F32),
+            pltpu.VMEM((3, 9 * CH + 8, 128), F32),
             pltpu.VMEM((2, 3, 4096, 128), BF16),
             pltpu.VMEM((4, 3, 2048, 128), BF16),
             pltpu.VMEM((4, 3, 3, 512, 128), BF16),
@@ -617,6 +653,7 @@
             pltpu.VMEM((4, CELLS, CH), BF16),
             pltpu.VMEM((4, 576, CH), BF16),
             pltpu.VMEM((4, 704, CH), BF16),
+            pltpu.SemaphoreType.DMA((4,)),
             pltpu.SemaphoreType.DMA((4,)),
             pltpu.SemaphoreType.DMA((4, 8)),
             pltpu.SemaphoreType.DMA((4, 8)),
@@ -632,9 +669,9 @@
     )(inputs.reshape(CELLS, CH), norm_gains, weights, cotangent.reshape(CELLS, CH))
     shape = (ROWS, COLS, CH)
     return (
-        out.reshape(shape),
-        input_grad.reshape(shape),
-        shares[:, :CHUNK].reshape(4, CHUNK * CH),
+        inputs.astype(F32) + out.reshape(shape),
+        cotangent + input_grad.reshape(shape),
+        shares,
     )
 
 

time: 144 us -> 131 us (0.910)
  Pallas kernels: 138 us -> 126 us
  local copies, waits for them, and re-layouts: 5.84 us -> 1.59 us
  other arithmetic: 0 us -> 2.99 us
    pallas_call x1, Pallas kernels: 138 us -> 126 us  [body(): pl.pallas_call(kernel, out_shape=(jax.ShapeDtypeStruct((CELLS, CH), F32),...]
    unnamed x4 -> x1, local copies, waits for them, and re-layouts: 5.84 us -> 1.59 us
    add x0 -> x1, other arithmetic: none -> 2.99 us  [body(): cotangent + input_grad.reshape(shape)]
where the time goes in v2:
time: 131 us
  Pallas kernels  126 us (96%)
  other arithmetic  2.99 us (2%)
  local copies, waits for them, and re-layouts  1.59 us (1%)
    pallas_call x1, Pallas kernels, body(): pl.pallas_call(kernel, out_shape=(jax.ShapeDtypeStruct((CELLS, CH), F32),...  126 us
    add x1, other arithmetic, body(): cotangent + input_grad.reshape(shape)  2.99 us

profile of v2, /device:TPU:0, one launch (start us, length us, event | category | flops | bytes accessed | tf_op | source)
XLA Modules:
  0.0 131.1 jit_solution(16598503355337018274)
XLA Ops:
  0.6 125.9 %shard_map.67 = (f32[512,384]{1,0:T(8,128)}, f32[512,384]{1,0:T(8,128)}, f32[4,10368]{1,0:T(4,128)}) custom-call(bf16[512,384]{1,0:T(8,128)(2,1)} %bitcast.7, f32[4,384]{1,0:T(4,128)} %gains.1, bf16[4,3456,384]{2,1,0:T(8,128)(2,1)} %w_hbm.1, f32[512,384]{1,0:T(8,128)} %bitcast.6), custom_call_target="tpu_custom_call" | custom-call | flops 16300000256 | bytes 15000000 | tf_op jit(solution)/shard_map/pallas_call | solution.py:625
  126.6 3.0 %bitcast_add_fusion = (f32[64,8,384]{2,1,0:T(8,128)}, f32[64,8,384]{2,1,0:T(8,128)}) fusion(f32[64,8,384]{2,1,0:T(8,128)} %param.7, f32[512,384]{1,0:T(8,128)} %get-tuple-element.7, f32[512,384]{1,0:T(8,128)} %get-tuple-element.6, bf16[64,8,384]{2,1,0:T(8,128)(2,1)} %param.4), kind=kLoop, calls=%fused_computation | loop fusion | flops 589824 | bytes 4325376 | tf_op jit(solution)/shard_map/add | solution.py:673
  129.5 1.6 %copy.8 = f32[4,10368]{1,0:T(4,128)} copy(f32[4,10368]{1,0:T(4,128)} %get-tuple-element.16) | data formatting | bytes 331776

commit v3 on v2

--- a/solution.py
+++ b/solution.py
@@ -306,13 +306,14 @@
     def plane_sent(slot):
         plane_wait(slot, as_sem)
 
-    def to_far(slot, load):
+    def to_far(slot, load, now=True):
         @pl.loop(0, 32)
         def _(q):
             both = jnp.concatenate([load(rows(q * 8, 8, 8)), load(rows(q * 8 + 256, 8, 8))], axis=0)
             AS[slot, rows(q * 16, 16), :] = both.astype(BF16)
 
-        plane_send(slot)
+        if now:
+            plane_send(slot)
 
     def at_far(slot, store):
         plane_wait(slot, ar_sem)
@@ -344,7 +345,7 @@
 
     def sibling_copy(k, p):
         return pltpu.make_async_remote_copy(
-            src_ref=SB.at[k % 2, p, rows((1 - core) * 2048, 2048)],
+            src_ref=SB.at[k % 3, p, rows((1 - core) * 2048, 2048)],
             dst_ref=R0.at[k, p],
             send_sem=rs_sem.at[k, p, 0],
             recv_sem=rr_sem.at[k, p, 0],
@@ -364,19 +365,34 @@
         base, size = held(p, level - 1)
         size = size // 4
         to = (here[axis] + step) & 3
-        land = (None, L1, L2, L3)[level]
+        land = (None, None, L2, L3)[level]
         return pltpu.make_async_remote_copy(
-            src_ref=SB.at[k % 2, p, rows((base + to * size) * 32, size * 32)],
+            src_ref=SB.at[k % 3, p, rows((base + to * size) * 32, size * 32)],
             dst_ref=land.at[k, p, step - 1],
-            send_sem=rs_sem.at[k, p, level * 3 - 3 + step],
-            recv_sem=rr_sem.at[k, p, level * 3 - 3 + step],
+            send_sem=rs_sem.at[k, p, level * 3 + step],
+            recv_sem=rr_sem.at[k, p, level * 3 + step],
             device_id=device(core, {**here, axis: to}),
             device_id_type=MESH,
         )
 
+    HOPS = ((2, 0, 1), (2, 1, 3), (1, 1, 1), (3, 0, 3), (1, 0, 1), (3, 1, 3))
+
+    def ring_copy(k, p, slot):
+        axis = ORDERS[p][0]
+        of, half, by = HOPS[slot]
+        start = core * 2048 + ((here[axis] + of) & 3) * 512 + half * 256
+        return pltpu.make_async_remote_copy(
+            src_ref=SB.at[k % 3, p, rows(start, 256)],
+            dst_ref=L1.at[k, p, slot],
+            send_sem=rs_sem.at[k, p, 1 + slot],
+            recv_sem=rr_sem.at[k, p, 1 + slot],
+            device_id=device(core, {**here, axis: (here[axis] + by) & 3}),
+            device_id_type=MESH,
+        )
+
     def reduce_0(k):
-        if k < 2:
-            reduce_sent(k + 2)
+        if k == 0:
+            reduce_sent(3)
 
         @pl.loop(0, 2)
         def _(high):
@@ -393,7 +409,7 @@
                                 at = {"x": n % 4, "z": pair * 2 + n // 4, "y": high * 2 + low}
                                 a, b, c = (at[axis] for axis in ORDERS[p])
                                 to = half * 64 + a * 16 + b * 4 + c
-                                SB[k % 2, p, rows(to * 32, 32), :] = eight[pl.ds(CHUNK * n, 32), :].astype(BF16)
+                                SB[k % 3, p, rows(to * 32, 32), :] = eight[pl.ds(CHUNK * n, 32), :].astype(BF16)
 
         for p in range(3):
             sibling_copy(k, p).start()
@@ -401,7 +417,9 @@
     def reduce_sent(k):
         for p in range(3):
             sibling_copy(k, p).wait_send()
-            for level in (1, 2, 3):
+            for slot in range(6):
+                ring_copy(k, p, slot).wait_send()
+            for level in (2, 3):
                 for step in (1, 2, 3):
                     axis_copy(k, p, level, step).wait_send()
 
@@ -412,30 +430,45 @@
             @pl.loop(0, 4)
             def _(i, p=p):
                 own = rows(core * 2048 + i * 512, 512)
-                SB[k % 2, p, own, :] = SB[k % 2, p, own, :] + R0[k, p, rows(i * 512, 512), :]
-
-            for step in (2, 1, 3):
-                axis_copy(k, p, 1, step).start()
+                SB[k % 3, p, own, :] = SB[k % 3, p, own, :] + R0[k, p, rows(i * 512, 512), :]
+
+            for slot in range(4):
+                ring_copy(k, p, slot).start()
+
+    def reduce_via(k):
+        for p in range(3):
+            for slot in (0, 1):
+                ring_copy(k, p, slot).wait_recv()
+                of, half, _ = HOPS[4 + slot]
+                own = rows(core * 2048 + ((here[ORDERS[p][0]] + of) & 3) * 512 + half * 256, 256)
+                SB[k % 3, p, own, :] = SB[k % 3, p, own, :] + L1[k, p, slot]
+                ring_copy(k, p, 4 + slot).start()
 
     def gathered(k, p, level, part, start):
-        land = (None, L1, L2, L3)[level]
+        land = (None, None, L2, L3)[level]
         base, _ = held(p, level)
-        total = SB[k % 2, p, rows(base * 32 + start, part), :].astype(F32)
+        total = SB[k % 3, p, rows(base * 32 + start, part), :].astype(F32)
         for step in (1, 2, 3):
             total = total + land[k, p, step - 1, rows(start, part), :].astype(F32)
         return total
 
     def reduce_next(k, level):
         for p in range(3):
-            for step in (1, 2, 3):
-                axis_copy(k, p, level, step).wait_recv()
             base, size = held(p, level)
-            part = min(256, size * 32)
-
-            @pl.loop(0, size * 32 // part)
-            def _(i, p=p, base=base):
-                total = gathered(k, p, level, part, i * part)
-                SB[k % 2, p, rows(base * 32 + i * part, part), :] = total.astype(BF16)
+            if level == 1:
+                for slot in (2, 3, 4, 5):
+                    ring_copy(k, p, slot).wait_recv()
+                for half, arrived in ((0, (3, 4)), (1, (2, 5))):
+                    own = rows(base * 32 + half * 256, 256)
+                    total = SB[k % 3, p, own, :].astype(F32)
+                    for slot in arrived:
+                        total = total + L1[k, p, slot].astype(F32)
+                    SB[k % 3, p, own, :] = total.astype(BF16)
+            else:
+                for step in (1, 2, 3):
+                    axis_copy(k, p, level, step).wait_recv()
+                total = gathered(k, p, level, size * 32, 0)
+                SB[k % 3, p, rows(base * 32, size * 32), :] = total.astype(BF16)
 
             for step in (2, 1, 3):
                 axis_copy(k, p, level + 1, step).start()
@@ -458,7 +491,7 @@
     pl.semaphore_wait(barrier, greeted)
     halo_send(0, 1)
     load_cot.wait()
-    to_far(0, lambda at: CT[at, :])
+    to_far(0, lambda at: CT[at, :], now=False)
     turn(0)
     loads[0].wait()
     halo_receive(0, 1)
@@ -493,6 +526,7 @@
         S[3, at, :] = values
 
     at_far(1, store_stream)
+    plane_send(0)
 
     act(2, 3, far_put)
     far_versions(1)
@@ -540,9 +574,9 @@
         S[6, at, :] = S[6, at, :] + pulled_back
 
     pull(3, far_3)
+    reduce_1(3)
     put_gradient(6, far_put)
     far_versions(1)
-    reduce_1(3)
     convolve(2, 64, -1, keep_d_act)
 
     def far_2(chunk, at, pulled_back):
@@ -550,7 +584,7 @@
 
     pull(2, far_2)
     to_near(3, lambda at: S[5, at, :])
-    reduce_next(3, 1)
+    reduce_via(3)
     kernel_gradient(2, 64)
     reduce_0(2)
 
@@ -568,10 +602,10 @@
     at_near(3, store_near_gradient)
     put_gradient(6, lambda chunk, values: near_put(4, chunk, values))
     halo_send(2, 4)
-    reduce_next(3, 2)
-    reduce_1(2)
+    reduce_next(3, 1)
     halo_receive(2, 4)
     near_versions(4)
+    reduce_1(2)
     convolve(1, 32, -1, keep_d_act)
 
     def near_1(chunk, at, pulled_back):
@@ -581,27 +615,31 @@
 
     pull(1, near_1)
     halo_send(3, 1)
-    reduce_last(3)
-    reduce_next(2, 1)
+    reduce_next(3, 2)
+    reduce_via(2)
     kernel_gradient(1, 32)
     reduce_0(1)
+    reduce_next(2, 1)
     halo_receive(3, 1)
     near_versions(1)
     kernel_gradient(0, 8)
-    reduce_next(2, 2)
     reduce_1(1)
-    reduce_last(2)
+    reduce_last(3)
     reduce_0(0)
     convolve(0, 8, -1, keep_d_act)
 
     def near_0(chunk, at, pulled_back):
         S[5, at, :] = S[5, at, :] + pulled_back
 
-    reduce_next(1, 1)
+    reduce_via(1)
+    reduce_next(2, 2)
+    reduce_1(0)
     pull(0, near_0)
     save_ig = pltpu.make_async_copy(S.at[5], ig, io_sem.at[3])
     save_ig.start()
-    reduce_1(0)
+    reduce_next(1, 1)
+    reduce_via(0)
+    reduce_last(2)
     reduce_next(1, 2)
     reduce_next(0, 1)
     reduce_last(1)
@@ -611,8 +649,8 @@
     save_out.wait()
     save_ig.wait()
 
-    reduce_sent(1)
-    reduce_sent(0)
+    for k in (2, 1, 0):
+        reduce_sent(k)
     for slot in range(4):
         plane_sent(slot)
     for slot, d in enumerate((1, 4, 4, 1)):
@@ -644,9 +682,9 @@
             pltpu.VMEM((3, 1024, CH), BF16),
             pltpu.VMEM((3, CELLS, CH), BF16),
             pltpu.VMEM((3, 9 * CH + 8, 128), F32),
-            pltpu.VMEM((2, 3, 4096, 128), BF16),
+            pltpu.VMEM((3, 3, 4096, 128), BF16),
             pltpu.VMEM((4, 3, 2048, 128), BF16),
-            pltpu.VMEM((4, 3, 3, 512, 128), BF16),
+            pltpu.VMEM((4, 3, 6, 256, 128), BF16),
             pltpu.VMEM((4, 3, 3, 128, 128), BF16),
             pltpu.VMEM((4, 3, 3, 32, 128), BF16),
             pltpu.VMEM((4, CELLS, CH), BF16),
@@ -659,8 +697,8 @@
             pltpu.SemaphoreType.DMA((4, 8)),
             pltpu.SemaphoreType.DMA((4,)),
             pltpu.SemaphoreType.DMA((4,)),
-            pltpu.SemaphoreType.DMA((4, 3, 10)),
-            pltpu.SemaphoreType.DMA((4, 3, 10)),
+            pltpu.SemaphoreType.DMA((4, 3, 13)),
+            pltpu.SemaphoreType.DMA((4, 3, 13)),
         ],
         compiler_params=pltpu.CompilerParams(
             collective_id=0, has_side_effects=True, vmem_limit_bytes=64 * 1024 * 1024

time: 131 us -> 126 us (0.962)
  Pallas kernels: 126 us -> 120 us
    pallas_call x1, Pallas kernels: 126 us -> 120 us  [body(): pl.pallas_call(kernel, out_shape=(jax.ShapeDtypeStruct((CELLS, CH), F32),...]
where the time goes in v3:
time: 126 us; the launch traced here: 125 us
  Pallas kernels  120 us (95%)
  other arithmetic  2.99 us (2%)
  local copies, waits for them, and re-layouts  1.59 us (1%)
    pallas_call x1, Pallas kernels, body(): pl.pallas_call(kernel, out_shape=(jax.ShapeDtypeStruct((CELLS, CH), F32),...  120 us
    add x1, other arithmetic, body(): cotangent + input_grad.reshape(shape)  2.99 us

profile of v3, /device:TPU:0, one launch (start us, length us, event | category | flops | bytes accessed | tf_op | source)
XLA Modules:
  0.0 125.5 jit_solution(11902286640293847875)
XLA Ops:
  0.6 120.3 %shard_map.67 = (f32[512,384]{1,0:T(8,128)}, f32[512,384]{1,0:T(8,128)}, f32[4,10368]{1,0:T(4,128)}) custom-call(bf16[512,384]{1,0:T(8,128)(2,1)} %bitcast.7, f32[4,384]{1,0:T(4,128)} %gains.1, bf16[4,3456,384]{2,1,0:T(8,128)(2,1)} %w_hbm.1, f32[512,384]{1,0:T(8,128)} %bitcast.6), custom_call_target="tpu_custom_call" | custom-call | flops 16300000256 | bytes 15000000 | tf_op jit(solution)/shard_map/pallas_call | solution.py:663
  120.9 3.0 %bitcast_add_fusion = (f32[64,8,384]{2,1,0:T(8,128)}, f32[64,8,384]{2,1,0:T(8,128)}) fusion(f32[64,8,384]{2,1,0:T(8,128)} %param.7, f32[512,384]{1,0:T(8,128)} %get-tuple-element.7, f32[512,384]{1,0:T(8,128)} %get-tuple-element.6, bf16[64,8,384]{2,1,0:T(8,128)(2,1)} %param.4), kind=kLoop, calls=%fused_computation | loop fusion | flops 589824 | bytes 4325376 | tf_op jit(solution)/shard_map/add | solution.py:711
  123.9 1.6 %copy.8 = f32[4,10368]{1,0:T(4,128)} copy(f32[4,10368]{1,0:T(4,128)} %get-tuple-element.16) | data formatting | bytes 331776

commit v4 on v3

--- a/solution.py
+++ b/solution.py
@@ -64,7 +64,7 @@
 
 def kernel(
     x_hbm, gains, w_hbm, cot_hbm, out, ig, wg_out,
-    W, X, CT, S, D, UN, IV, AT, F, V, U, G, SB, R0, L1, L2, L3, AS, AL, HS, HL,
+    W, X, CT, S, D, UN, IV, AT, F, V, U, G, SB, TB, R0, L1, L2, L3, AS, AL, HS, HL,
     w_sem, io_sem, hs_sem, hr_sem, as_sem, ar_sem, rs_sem, rr_sem,
 ):
     gx, gy = lax.axis_index("gx"), lax.axis_index("gy")
@@ -200,7 +200,7 @@
                 put(lambda at, size: jnp.zeros((size, CH), F32))
 
     def near_versions(d):
-        @pl.loop(0, (ROWS + 2 * d) // 2)
+        @pl.loop(0, (ROWS + 2 * d) // 2, unroll=3 if d == 1 else 4)
         def _(i):
             pair = [padded(rows((2 * i + n) * PITCH, PITCH, 8)) for n in (0, 1)]
             for c in (-1, 0, 1):
@@ -209,7 +209,7 @@
 
         if d == 1:
 
-            @pl.loop(0, ROWS // 2)
+            @pl.loop(0, ROWS // 2, unroll=4)
             def _(i):
                 pair = [padded(rows((2 * i + n + 1) * PITCH, PITCH, 8)) for n in (0, 1)]
                 for c in (-1, 0, 1):
@@ -228,7 +228,7 @@
             V[c + 1, pl.ds(0, s * 64), :] = jnp.zeros((s * 64, CH), BF16)
             V[c + 1, pl.ds((8 + s) * 64, s * 64), :] = jnp.zeros((s * 64, CH), BF16)
 
-            @pl.loop(0, 8)
+            @pl.loop(0, 8, unroll=4)
             def _(i, c=c):
                 V[c + 1, rows((i + s) * 64, 64), :] = padded(rows(i * 128 + 32 + c * s * 8, 64, 8)).astype(BF16)
 
@@ -262,7 +262,7 @@
     def act(k, slot, put):
         gain = gains[k : k + 1, :]
 
-        @pl.loop(0, 8)
+        @pl.loop(0, 8, unroll=4)
         def _(chunk):
             unit, inverse = normed(S[slot, rows(chunk * 64, 64), :])
             UN[k, rows(chunk * 64, 64), :] = unit
@@ -307,7 +307,7 @@
         plane_wait(slot, as_sem)
 
     def to_far(slot, load, now=True):
-        @pl.loop(0, 32)
+        @pl.loop(0, 32, unroll=4)
         def _(q):
             both = jnp.concatenate([load(rows(q * 8, 8, 8)), load(rows(q * 8 + 256, 8, 8))], axis=0)
             AS[slot, rows(q * 16, 16), :] = both.astype(BF16)
@@ -318,7 +318,7 @@
     def at_far(slot, store):
         plane_wait(slot, ar_sem)
 
-        @pl.loop(0, 32)
+        @pl.loop(0, 32, unroll=4)
         def _(q):
             both = AL[slot, rows(q * 16, 16), :].astype(F32)
             base = ((q >> 3) * 16 + (q & 7)) * 8
@@ -326,7 +326,7 @@
             store(rows(base + 64, 8, 8), both[8:16])
 
     def to_near(slot, load):
-        @pl.loop(0, 32)
+        @pl.loop(0, 32, unroll=4)
         def _(q):
             base = ((q >> 3) * 16 + (q & 7)) * 8
             both = jnp.concatenate([load(rows(base, 8, 8)), load(rows(base + 64, 8, 8))], axis=0)
@@ -337,7 +337,7 @@
     def at_near(slot, store):
         plane_wait(slot, ar_sem)
 
-        @pl.loop(0, 32)
+        @pl.loop(0, 32, unroll=4)
         def _(q):
             both = AL[slot, rows(q * 16, 16), :].astype(F32)
             store(rows(q * 8, 8, 8), both[0:8])
@@ -365,10 +365,13 @@
         base, size = held(p, level - 1)
         size = size // 4
         to = (here[axis] + step) & 3
-        land = (None, None, L2, L3)[level]
+        if level == 2:
+            source = SB.at[k % 3, p, rows((base + to * size) * 32, size * 32)]
+        else:
+            source = TB.at[k, p, rows(to * 32, 32)]
         return pltpu.make_async_remote_copy(
-            src_ref=SB.at[k % 3, p, rows((base + to * size) * 32, size * 32)],
-            dst_ref=land.at[k, p, step - 1],
+            src_ref=source,
+            dst_ref=(L2 if level == 2 else L3).at[k, p, step - 1],
             send_sem=rs_sem.at[k, p, level * 3 + step],
             recv_sem=rr_sem.at[k, p, level * 3 + step],
             device_id=device(core, {**here, axis: to}),
@@ -444,14 +447,6 @@
                 SB[k % 3, p, own, :] = SB[k % 3, p, own, :] + L1[k, p, slot]
                 ring_copy(k, p, 4 + slot).start()
 
-    def gathered(k, p, level, part, start):
-        land = (None, None, L2, L3)[level]
-        base, _ = held(p, level)
-        total = SB[k % 3, p, rows(base * 32 + start, part), :].astype(F32)
-        for step in (1, 2, 3):
-            total = total + land[k, p, step - 1, rows(start, part), :].astype(F32)
-        return total
-
     def reduce_next(k, level):
         for p in range(3):
             base, size = held(p, level)
@@ -467,8 +462,10 @@
             else:
                 for step in (1, 2, 3):
                     axis_copy(k, p, level, step).wait_recv()
-                total = gathered(k, p, level, size * 32, 0)
-                SB[k % 3, p, rows(base * 32, size * 32), :] = total.astype(BF16)
+                total = SB[k % 3, p, rows(base * 32, size * 32), :].astype(F32)
+                for step in (1, 2, 3):
+                    total = total + L2[k, p, step - 1].astype(F32)
+                TB[k, p] = total
 
             for step in (2, 1, 3):
                 axis_copy(k, p, level + 1, step).start()
@@ -477,7 +474,10 @@
         for p in range(3):
             for step in (1, 2, 3):
                 axis_copy(k, p, 3, step).wait_recv()
-            total = gathered(k, p, 3, 32, 0) * (1.0 / 256.0)
+            total = TB[k, p, rows(here[ORDERS[p][2]] * 32, 32, 8), :]
+            for step in (1, 2, 3):
+                total = total + L3[k, p, step - 1]
+            total = total * (1.0 / 256.0)
             for r in range(CHUNK):
                 wg_out[k : k + 1, r * CH + p * 128 : r * CH + (p + 1) * 128] = total[r : r + 1]
 
@@ -548,7 +548,7 @@
     at_far(0, store_gradient)
 
     def put_gradient(slot, put):
-        @pl.loop(0, 8)
+        @pl.loop(0, 8, unroll=4)
         def _(chunk):
             put(chunk, S[slot, rows(chunk * 64, 64), :].astype(BF16).astype(F32))
 
@@ -558,7 +558,7 @@
     def pull(k, finish):
         gain = gains[k : k + 1, :]
 
-        @pl.loop(0, 8)
+        @pl.loop(0, 8, unroll=4)
         def _(chunk):
             at = rows(chunk * 64, 64)
             finish(chunk, at, pulled(UN[k, at, :], IV[k, at, :][:, :1], gain, D[at, :]))
@@ -655,6 +655,15 @@
         plane_sent(slot)
     for slot, d in enumerate((1, 4, 4, 1)):
         halo_sent(slot, d)
+
+
+def closing(x_ref, grown, cot_ref, pulled_back, shares, out, ig, wg):
+    out[...] = x_ref[...].astype(F32) + grown[...]
+    ig[...] = cot_ref[...] + pulled_back[...]
+
+    @pl.when(pl.program_id(0) == 0)
+    def _():
+        wg[...] = shares[...]
 
 
 def body(inputs, norm_gains, weights, cotangent):
@@ -683,10 +692,11 @@
             pltpu.VMEM((3, CELLS, CH), BF16),
             pltpu.VMEM((3, 9 * CH + 8, 128), F32),
             pltpu.VMEM((3, 3, 4096, 128), BF16),
+            pltpu.VMEM((4, 3, 128, 128), F32),
             pltpu.VMEM((4, 3, 2048, 128), BF16),
             pltpu.VMEM((4, 3, 6, 256, 128), BF16),
             pltpu.VMEM((4, 3, 3, 128, 128), BF16),
-            pltpu.VMEM((4, 3, 3, 32, 128), BF16),
+            pltpu.VMEM((4, 3, 3, 32, 128), F32),
             pltpu.VMEM((4, CELLS, CH), BF16),
             pltpu.VMEM((4, CELLS, CH), BF16),
             pltpu.VMEM((4, 576, CH), BF16),
@@ -705,12 +715,22 @@
         ),
         cost_estimate=pl.CostEstimate(flops=16_300_000_000, bytes_accessed=15_000_000, transcendentals=4_000_000),
     )(inputs.reshape(CELLS, CH), norm_gains, weights, cotangent.reshape(CELLS, CH))
+    part = pl.BlockSpec((CELLS // 4, CH), lambda i: (i, 0))
+    whole = pl.BlockSpec((4, CHUNK * CH), lambda i: (0, 0))
+    out, input_grad, shares = pl.pallas_call(
+        closing,
+        grid=(4,),
+        out_shape=(
+            jax.ShapeDtypeStruct((CELLS, CH), F32),
+            jax.ShapeDtypeStruct((CELLS, CH), F32),
+            jax.ShapeDtypeStruct((4, CHUNK * CH), F32),
+        ),
+        in_specs=[part, part, part, part, whole],
+        out_specs=(part, part, whole),
+        cost_estimate=pl.CostEstimate(flops=400_000, bytes_accessed=4_600_000, transcendentals=0),
+    )(inputs.reshape(CELLS, CH), out, cotangent.reshape(CELLS, CH), input_grad, shares)
     shape = (ROWS, COLS, CH)
-    return (
-        inputs.astype(F32) + out.reshape(shape),
-        cotangent + input_grad.reshape(shape),
-        shares,
-    )
+    return out.reshape(shape), input_grad.reshape(shape), shares
 
 
 def solution(mesh):

time: 126 us -> 118 us (0.937)
  Pallas kernels: 120 us -> 117 us
  other arithmetic: 2.99 us -> 0 us
  local copies, waits for them, and re-layouts: 1.59 us -> 0 us
    pallas_call x1, Pallas kernels: 120 us -> 112 us  [body(): pl.pallas_call(kernel, out_shape=(jax.ShapeDtypeStruct((CELLS, CH), F32),...]
    pallas_call x0 -> x1, Pallas kernels: none -> 4.15 us  [body(): pl.pallas_call(closing, grid=(4,), out_shape=(jax.ShapeDtypeStruct((CELLS...]
    add x1 -> x0, other arithmetic: 2.99 us -> none  [body(): cotangent + input_grad.reshape(shape)]
    unnamed x1 -> x0, local copies, waits for them, and re-layouts: 1.59 us -> none
where the time goes in v4:
time: 118 us; the launch traced here: 117 us
  Pallas kernels  117 us (99%)
    pallas_call x1, Pallas kernels, body(): pl.pallas_call(kernel, out_shape=(jax.ShapeDtypeStruct((CELLS, CH), F32),...  112 us
    pallas_call x1, Pallas kernels, body(): pl.pallas_call(closing, grid=(4,), out_shape=(jax.ShapeDtypeStruct((CELLS...  4.15 us

profile of v4, /device:TPU:0, one launch (start us, length us, event | category | flops | bytes accessed | tf_op | source)
XLA Modules:
  0.0 117.4 jit_solution(6936504578110432270)
XLA Ops:
  0.6 112.4 %shard_map.67 = (f32[512,384]{1,0:T(8,128)}, f32[512,384]{1,0:T(8,128)}, f32[4,10368]{1,0:T(4,128)}) custom-call(bf16[512,384]{1,0:T(8,128)(2,1)} %bitcast.6, f32[4,384]{1,0:T(4,128)} %gains.1, bf16[4,3456,384]{2,1,0:T(8,128)(2,1)} %w_hbm.1, f32[512,384]{1,0:T(8,128)} %bitcast.4), custom_call_target="tpu_custom_call" | custom-call | flops 16300000256 | bytes 15000000 | tf_op jit(solution)/shard_map/pallas_call | solution.py:672
  113.1 4.1 %shard_map.68 = (f32[512,384]{1,0:T(8,128)}, f32[512,384]{1,0:T(8,128)}, f32[4,10368]{1,0:T(4,128)}) custom-call(bf16[512,384]{1,0:T(8,128)(2,1)} %bitcast.7, f32[512,384]{1,0:T(8,128)} %get-tuple-element.9.grown, f32[512,384]{1,0:T(8,128)} %bitcast.5, f32[512,384]{1,0:T(8,128)} %get-tuple-element.10.pulled_back, f32[4,10368]{1,0:T(4,128)} %get-tuple-element.11.shares), custom_call_target="tpu_custom_call" | custom-call | flops 400000 | bytes 4600000 | tf_op jit(solution)/shard_map/pallas_call | solution.py:720

commit v5 on v4

--- a/solution.py
+++ b/solution.py
@@ -225,8 +225,9 @@
 
     def far_versions(s):
         for c in (-1, 0, 1):
-            V[c + 1, pl.ds(0, s * 64), :] = jnp.zeros((s * 64, CH), BF16)
-            V[c + 1, pl.ds((8 + s) * 64, s * 64), :] = jnp.zeros((s * 64, CH), BF16)
+            if s == 1:
+                V[c + 1, pl.ds(0, 64), :] = jnp.zeros((64, CH), BF16)
+                V[c + 1, pl.ds(576, 64), :] = jnp.zeros((64, CH), BF16)
 
             @pl.loop(0, 8, unroll=4)
             def _(i, c=c):
@@ -242,27 +243,24 @@
                 found.append((V.at[c + 1], (1 + r) * step))
         return found
 
-    BLOCK = 256
-
     def convolve(k, step, sign, finish):
         found = sources(step, sign)
-
-        @pl.loop(0, CELLS // BLOCK)
-        def _(m):
-            left = jnp.concatenate(
-                [ref[rows(m * BLOCK + start, BLOCK), :] for ref, start in found], axis=1
-            )
+        pieces = ((0, CELLS, 0, 9),)
+        if k == 3:
+            pieces = ((0, 256, 3, 9), (256, 256, 0, 6)) if sign == 1 else ((0, 256, 0, 6), (256, 256, 3, 9))
+        for at, size, first, last in pieces:
+            left = jnp.concatenate([ref[pl.ds(at + start, size), :] for ref, start in found[first:last]], axis=1)
             if sign == 1:
-                result = jnp.dot(left, W[k], preferred_element_type=F32)
+                result = jnp.dot(left, W[k, first * CH : last * CH, :], preferred_element_type=F32)
             else:
-                right = jnp.concatenate([W[k, t * CH : (t + 1) * CH, :] for t in range(9)], axis=1)
+                right = jnp.concatenate([W[k, t * CH : (t + 1) * CH, :] for t in range(first, last)], axis=1)
                 result = lax.dot_general(left, right, (((1,), (1,)), ((), ())), preferred_element_type=F32)
-            finish(rows(m * BLOCK, BLOCK), result)
+            finish(pl.ds(at, size), result)
 
     def act(k, slot, put):
         gain = gains[k : k + 1, :]
 
-        @pl.loop(0, 8, unroll=4)
+        @pl.loop(0, 8, unroll=8)
         def _(chunk):
             unit, inverse = normed(S[slot, rows(chunk * 64, 64), :])
             UN[k, rows(chunk * 64, 64), :] = unit
@@ -276,11 +274,14 @@
 
     def kernel_gradient(k, step):
         found = sources(step, -1)
-        for first in (0, 2, 4, 6, 8):
-            pair = found[first : first + 2]
-            right = jnp.concatenate([ref[pl.ds(start, CELLS), :] for ref, start in pair], axis=1)
-            both = jnp.dot(AT[k], right, preferred_element_type=F32)
-            for n in range(len(pair)):
+        groups = tuple((first, 2, 0, CELLS) for first in (0, 2, 4, 6)) + ((8, 1, 0, CELLS),)
+        if k == 3:
+            groups = ((0, 2, 0, 256), (2, 1, 0, 256), (3, 2, 0, CELLS), (5, 1, 0, CELLS), (6, 2, 256, 256), (8, 1, 256, 256))
+        for first, count, at, size in groups:
+            taps = found[first : first + count]
+            right = jnp.concatenate([ref[pl.ds(at + start, size), :] for ref, start in taps], axis=1)
+            both = jnp.dot(AT[k, :, at : at + size], right, preferred_element_type=F32)
+            for n in range(count):
                 for p in range(3):
                     G[p, pl.ds((first + n) * CH, CH), :] = both[:, n * CH + p * 128 : n * CH + (p + 1) * 128]
 
@@ -403,7 +404,7 @@
             def _(half):
                 @pl.loop(0, 2)
                 def _(low):
-                    @pl.loop(0, 2)
+                    @pl.loop(0, 2, unroll=2)
                     def _(pair):
                         first = (high * 4 + half * 2 + low) * 16 + pair * 8
                         for p in range(3):
@@ -543,7 +544,7 @@
     turn(3)
 
     def store_gradient(at, values):
-        S[6, at, :] = values
+        S[1, at, :] = values
 
     at_far(0, store_gradient)
 
@@ -558,12 +559,12 @@
     def pull(k, finish):
         gain = gains[k : k + 1, :]
 
-        @pl.loop(0, 8, unroll=4)
+        @pl.loop(0, 8, unroll=8)
         def _(chunk):
             at = rows(chunk * 64, 64)
             finish(chunk, at, pulled(UN[k, at, :], IV[k, at, :][:, :1], gain, D[at, :]))
 
-    put_gradient(6, far_put)
+    put_gradient(1, far_put)
     far_versions(4)
     kernel_gradient(3, 256)
     reduce_0(3)
@@ -571,11 +572,11 @@
 
     def far_3(chunk, at, pulled_back):
         S[5, at, :] = pulled_back
-        S[6, at, :] = S[6, at, :] + pulled_back
+        S[1, at, :] = S[1, at, :] + pulled_back
 
     pull(3, far_3)
     reduce_1(3)
-    put_gradient(6, far_put)
+    put_gradient(1, far_put)
     far_versions(1)
     convolve(2, 64, -1, keep_d_act)
 
@@ -596,11 +597,11 @@
     save_out.start()
 
     def store_near_gradient(at, values):
-        S[6, at, :] = CT[at, :] + values
+        S[1, at, :] = CT[at, :] + values
         S[5, at, :] = values
 
     at_near(3, store_near_gradient)
-    put_gradient(6, lambda chunk, values: near_put(4, chunk, values))
+    put_gradient(1, lambda chunk, values: near_put(4, chunk, values))
     halo_send(2, 4)
     reduce_next(3, 1)
     halo_receive(2, 4)
@@ -609,7 +610,7 @@
     convolve(1, 32, -1, keep_d_act)
 
     def near_1(chunk, at, pulled_back):
-        total = S[6, at, :] + pulled_back
+        total = S[1, at, :] + pulled_back
         S[5, at, :] = S[5, at, :] + pulled_back
         near_put(1, chunk, total.astype(BF16).astype(F32))
 
@@ -682,7 +683,7 @@
             pltpu.VMEM((4, 9 * CH, CH), BF16),
             pltpu.VMEM((CELLS, CH), BF16),
             pltpu.VMEM((CELLS, CH), F32),
-            pltpu.VMEM((7, CELLS, CH), F32),
+            pltpu.VMEM((6, CELLS, CH), F32),
             pltpu.VMEM((CELLS, CH), F32),
             pltpu.VMEM((4, CELLS, CH), F32),
             pltpu.VMEM((4, CELLS, 128), F32),

time: 118 us -> 115 us (0.975)
  Pallas kernels: 117 us -> 114 us
    pallas_call x1, Pallas kernels: 112 us -> 110 us  [body(): pl.pallas_call(kernel, out_shape=(jax.ShapeDtypeStruct((CELLS, CH), F32),...]
where the time goes in v5:
time: 115 us
  Pallas kernels  114 us (99%)
    pallas_call x1, Pallas kernels, body(): pl.pallas_call(kernel, out_shape=(jax.ShapeDtypeStruct((CELLS, CH), F32),...  110 us
    pallas_call x1, Pallas kernels, body(): pl.pallas_call(closing, grid=(4,), out_shape=(jax.ShapeDtypeStruct((CELLS...  4.15 us

profile of v5, /device:TPU:0, one launch (start us, length us, event | category | flops | bytes accessed | tf_op | source)
XLA Modules:
  0.0 114.9 jit_solution(13645422922836474356)
XLA Ops:
  0.6 109.9 %shard_map.67 = (f32[512,384]{1,0:T(8,128)}, f32[512,384]{1,0:T(8,128)}, f32[4,10368]{1,0:T(4,128)}) custom-call(bf16[512,384]{1,0:T(8,128)(2,1)} %bitcast.6, f32[4,384]{1,0:T(4,128)} %gains.1, bf16[4,3456,384]{2,1,0:T(8,128)(2,1)} %w_hbm.1, f32[512,384]{1,0:T(8,128)} %bitcast.4), custom_call_target="tpu_custom_call" | custom-call | flops 16300000256 | bytes 15000000 | tf_op jit(solution)/shard_map/pallas_call | solution.py:673
  110.6 4.1 %shard_map.68 = (f32[512,384]{1,0:T(8,128)}, f32[512,384]{1,0:T(8,128)}, f32[4,10368]{1,0:T(4,128)}) custom-call(bf16[512,384]{1,0:T(8,128)(2,1)} %bitcast.7, f32[512,384]{1,0:T(8,128)} %get-tuple-element.9.grown, f32[512,384]{1,0:T(8,128)} %bitcast.5, f32[512,384]{1,0:T(8,128)} %get-tuple-element.10.pulled_back, f32[4,10368]{1,0:T(4,128)} %get-tuple-element.11.shares), custom_call_target="tpu_custom_call" | custom-call | flops 400000 | bytes 4600000 | tf_op jit(solution)/shard_map/pallas_call | solution.py:721
